TPU v7x, 32 devices: a whole 2x2x4 slice. The times are simulated.
32 devices in a mesh: grp: 2 (over x), cell: 16 (over z, y, core).
Axes of the slice: x: 2, y: 2, z: 4, core: 2. Of those that a mesh axis runs over, the one named last changes fastest.
Arguments:
- fields: bfloat16 [8192, 3, 8192], P(('grp', 'cell')), parts along dimension 0, may hold values from -6 to 6
- horiz: float32 [16384], P(('grp', 'cell')), parts along dimension 0, may hold values from 0.2 to 1
- vertical: float32 [16384], P(('grp', 'cell')), parts along dimension 0, may hold values from 1.5 to 6
- tilt_angle: float32 [16384], P(('grp', 'cell')), parts along dimension 0, may hold values from 0.2 to 1.4
- azimuth: float32 [16384], P(('grp', 'cell')), parts along dimension 0, may hold values from -3.140625 to 3.140625
- electrode_quads: int32 [4096, 4], P('grp'), parts along dimension 0, may hold values from 0 to 4095, as said below
Outputs:
- jacobian: bfloat16 [4096, 4, 8192], P('grp', None, 'cell'), parts along dimension 0
- coverage: float32 [16384], P(('grp', 'cell')), parts along dimension 0
There are 2 independent parts, one for each index of `grp`. A program takes and returns all parts, laid end to end along the dimension named above; each array names one. Nothing has to cross between parts.
Inputs may be any that keep to these rules, and one draw needn't show every extreme that they name: `electrode_quads`: each row names four different electrodes.
All inputs are finite; a program needn't handle non-finite values.
Results may differ from a plain program's by a relative error of at most 0.001.
Values may be sent and summed in bfloat16 or wider, within the bound.
No kernel may reach another device: no remote copies, remote signals or barrier semaphores. Data moves between devices by JAX's collectives and lax.ppermute only.
A program may use at most 192 MiB of HBM per device.

v0:
```python
import functools

import jax
import jax.numpy as jnp
from jax import lax
from jax.experimental import pallas as pl
from jax.experimental.pallas import tpu as pltpu
from jax.sharding import PartitionSpec as P

LANES = 128
SUBLANES = 8
UNROLL = 16
FILL_STEPS = 4
GROUP_ROWS = 512
SCALE_ROWS = 256
ROW_TILE = 8
KEEPS = (28, 30)
POOL = 5
PAD = 4
MIB = 1 << 20
VMEM_LIMIT = 60 * MIB
SENS_LIMIT = 32 * MIB
SCALE_LIMIT = 48 * MIB
NEAR_BYTES = 4 * MIB


def one_hots(quads_ref, column, high):
    index = quads_ref[pl.ds(column, 1), :]
    total = index.shape[1]
    upper = lax.broadcasted_iota(jnp.int32, (high, total), 0) == index // LANES
    lower = lax.broadcasted_iota(jnp.int32, (LANES, total), 0) == index % LANES
    return upper.astype(jnp.bfloat16), lower.astype(jnp.bfloat16)


def named_ranks(quads_ref, high, per, base):
    count = jnp.zeros((high, LANES), jnp.float32)
    for column in range(4):
        upper, lower = one_hots(quads_ref, column, high)
        count += lax.dot_general(upper, lower, (((1,), (1,)), ((), ())), preferred_element_type=jnp.float32)
    named = (count > 0).astype(jnp.bfloat16)

    def dot(a, b):
        return jnp.dot(a.astype(jnp.bfloat16), b.astype(jnp.bfloat16), preferred_element_type=jnp.float32)

    i, j = (lax.broadcasted_iota(jnp.int32, (LANES, LANES), d) for d in range(2))
    within = dot(named, i < j)
    lines = dot(named, jnp.ones((LANES, LANES), jnp.bfloat16))
    i, j = (lax.broadcasted_iota(jnp.int32, (high, high), d) for d in range(2))
    rank = jnp.where(count > 0, within + dot((j < i) & (j // per == i // per), lines), -1.0)
    over = jnp.maximum(dot(j // per == i // per, lines) - base, 0.0)
    ahead = dot((j // per < i // per) & (j % per == 0), over)
    slot = jnp.where(rank >= base, rank - base + ahead, -1.0)
    return rank, slot, ahead + over


def table_rows_kernel(quads_ref, place_ref, rows_ref):
    place = place_ref[...]
    coarse = jnp.floor(place * (1.0 / 16.0))
    fine = place - 16.0 * coarse
    for column in range(4):
        upper, lower = one_hots(quads_ref, column, place.shape[0])

        def pick(part):
            spread = lax.dot_general(
                part.astype(jnp.bfloat16), upper, (((0,), (0,)), ((), ())), preferred_element_type=jnp.float32
            )
            return jnp.sum(spread * lower.astype(jnp.float32), axis=0, keepdims=True)

        rows_ref[pl.ds(column, 1), :] = (pick(coarse) * 16.0 + pick(fine)).astype(jnp.int32) * PAD


def table_rows(quads, place):
    whole = pl.BlockSpec(memory_space=pltpu.VMEM)
    return pl.pallas_call(
        table_rows_kernel,
        in_specs=[whole, whole],
        out_specs=whole,
        out_shape=jax.ShapeDtypeStruct(quads.shape, jnp.int32),
        name="table_rows",
    )(quads, place)


def send_order_kernel(first, fields_ref, out_ref, held, in_sems, out_sems):
    shards, _, _, width = held.shape
    cell_dev = fields_ref.shape[2] // shards
    arrive = [
        pltpu.make_async_copy(fields_ref.at[:, :, pl.ds(d * cell_dev + first, width)], held.at[d], in_sems.at[d])
        for d in range(shards)
    ]
    leave = [pltpu.make_async_copy(held.at[d], out_ref.at[d], out_sems.at[d]) for d in range(shards)]
    for copy in arrive:
        copy.start()
    for d in range(shards):
        arrive[d].wait()
        leave[d].start()
    for copy in leave:
        copy.wait()


def choose_rows(choose, rank_ref):
    kept, owned = choose.shape
    me = lax.axis_index("cell")
    place = lax.broadcasted_iota(jnp.int32, (kept, LANES), 0).astype(jnp.float32)
    for k in range(owned // LANES):
        line = rank_ref[pl.ds(me * (owned // LANES) + k, 1), :]
        choose[:, k * LANES : (k + 1) * LANES] = (place == line).astype(choose.dtype)


def send_chosen(arrive, choose, held, packed, out_ref, out_sems):
    shards, comps = held.shape[:2]
    kept = packed.shape[2]

    def leave(d):
        return pltpu.make_async_copy(packed.at[d], out_ref.at[d], out_sems.at[d])

    @pl.loop(0, shards)
    def _(d):
        arrive(d).wait()
        for comp in range(comps):
            rows = jnp.dot(choose[pl.ds(0, kept), :], held[d, comp], preferred_element_type=jnp.float32)
            packed[d, comp] = rows.astype(packed.dtype)
        leave(d).start()

    @pl.loop(0, shards)
    def _(d):
        leave(d).wait()


def arrival(first, fields_ref, held, in_sems):
    shards, _, _, width = held.shape
    cell_dev = fields_ref.shape[2] // shards

    def arrive(d):
        lanes = pl.ds(pl.multiple_of(d * cell_dev + first, LANES), width)
        return pltpu.make_async_copy(fields_ref.at[:, :, lanes], held.at[d], in_sems.at[d])

    return arrive


def send_named_kernel(first, fields_ref, rank_ref, out_ref, held, packed, choose, in_sems, out_sems):
    arrive = arrival(first, fields_ref, held, in_sems)
    for d in range(held.shape[0]):
        arrive(d).start()
    choose_rows(choose, rank_ref)
    send_chosen(arrive, choose, held, packed, out_ref, out_sems)


def send_first_kernel(keeps, pool, fields_ref, quads_ref, *refs):
    out_refs, (rank_ref, slot_ref, place_ref, chosen_ref, held) = refs[: len(keeps)], refs[len(keeps) : len(keeps) + 5]
    packed, (choose, in_sems, out_sems) = refs[len(keeps) + 5 : -3], refs[-3:]
    arrive = arrival(0, fields_ref, held, in_sems)
    for d in range(held.shape[0]):
        arrive(d).start()
    shards, _, owned, _ = held.shape
    high, per = rank_ref.shape[0], owned // LANES
    rank, slot, taken = named_ranks(quads_ref, high, per, float(keeps[0]))
    rank_ref[...] = rank
    slot_ref[...] = slot
    most = (jnp.max(rank) + 1.0).astype(jnp.int32)
    pooled = (jnp.max(taken) <= pool).astype(jnp.int32)
    chosen = sum((most > kept).astype(jnp.int32) for kept in keeps[1:])
    chosen = (1 - pooled) * (1 + chosen)
    chosen_ref[0] = chosen
    owner = (lax.broadcasted_iota(jnp.int32, (high, LANES), 0) // per).astype(jnp.float32)
    place = jnp.where(slot < 0.0, owner * keeps[0] + rank, slot + shards * keeps[0])
    for k, kept in enumerate(keeps[1:]):
        place = jnp.where(chosen == k + 1, owner * kept + rank, place)
    place_ref[...] = place
    choose_rows(choose, rank_ref)
    for k, kept in enumerate(keeps):

        @pl.when(chosen == k)
        def _():
            send_chosen(arrive, choose, held, packed[k], out_refs[k], out_sems)

    @pl.when(chosen == len(keeps))
    def _():
        for d in range(held.shape[0]):
            arrive(d).wait()


def send_first(fields, quads, keeps, pool, shards, width):
    comps, owned, cells = fields.shape
    sent = [(shards, comps, kept, width) for kept in keeps]
    anywhere, whole = pl.BlockSpec(memory_space=pl.ANY), pl.BlockSpec(memory_space=pltpu.VMEM)
    table = jax.ShapeDtypeStruct((shards * owned // LANES, LANES), jnp.float32)
    *ready, rank, slot, place, chosen = pl.pallas_call(
        functools.partial(send_first_kernel, keeps, pool),
        in_specs=[anywhere, whole],
        out_specs=[anywhere] * len(keeps) + [whole] * 3 + [pl.BlockSpec(memory_space=pltpu.SMEM)],
        out_shape=[jax.ShapeDtypeStruct(shape, fields.dtype) for shape in sent]
        + [table] * 3
        + [jax.ShapeDtypeStruct((1,), jnp.int32)],
        scratch_shapes=[pltpu.VMEM((shards, comps, owned, width), fields.dtype)]
        + [pltpu.VMEM(shape, fields.dtype) for shape in sent]
        + [
            pltpu.VMEM((max(keeps), owned), fields.dtype),
            pltpu.SemaphoreType.DMA((shards,)),
            pltpu.SemaphoreType.DMA((shards,)),
        ],
        compiler_params=pltpu.CompilerParams(vmem_limit_bytes=VMEM_LIMIT),
        name="send_first",
    )(fields, quads)
    return ready, (rank, slot, place), chosen[0]


def send_order(fields, rank, kept, shards, first, width):
    comps, owned, cells = fields.shape
    held = (shards, comps, owned, width)
    sent = (shards, comps, kept, width)
    scratch = [pltpu.VMEM(held, fields.dtype)]
    in_specs, args = [pl.BlockSpec(memory_space=pl.ANY)], [fields]
    if rank is not None:
        scratch += [pltpu.VMEM(sent, fields.dtype), pltpu.VMEM((kept, owned), fields.dtype)]
        in_specs.append(pl.BlockSpec(memory_space=pltpu.VMEM))
        args.append(rank)
    return pl.pallas_call(
        functools.partial(send_order_kernel if rank is None else send_named_kernel, first),
        in_specs=in_specs,
        out_specs=pl.BlockSpec(memory_space=pl.ANY),
        out_shape=jax.ShapeDtypeStruct(sent, fields.dtype),
        scratch_shapes=scratch + [pltpu.SemaphoreType.DMA((shards,)), pltpu.SemaphoreType.DMA((shards,))],
        cost_estimate=pl.CostEstimate(flops=0, bytes_accessed=4 * comps * owned * width * shards, transcendentals=0),
        compiler_params=pltpu.CompilerParams(vmem_limit_bytes=VMEM_LIMIT),
        name="send_order",
    )(*args)


def sens_kernel(sources, fill_steps, group_rows, near, all_rows_ref, fields_ref, coef_ref, before_ref, *refs):
    sens_ref, sumsq_ref, table, picked, squares, rows_ref, rows_sem = refs[-7:]
    step = pl.program_id(0)
    rows_copy = pltpu.make_async_copy(all_rows_ref, rows_ref, rows_sem)

    @pl.when(step == 0)
    def _():
        rows_copy.start()

    @pl.when(step == fill_steps)
    def _():
        rows_copy.wait()
        if len(refs) > 7:
            pool_ref = refs[0]
            pool = pool_ref.shape[1]
            for comp in range(pool_ref.shape[0]):
                values = pool_ref[comp].astype(jnp.float32)
                table[pl.ds(table.shape[0] - pool * PAD + comp, pool, stride=PAD), :] = values

    owned = fields_ref.shape[2]
    batch_rows = SUBLANES * UNROLL
    total_rows = rows_ref.shape[0] // 4

    @pl.when(step < fill_steps)
    def _():
        for source in range(sources):
            place = step * sources + source
            for comp in range(fields_ref.shape[1]):
                values = fields_ref[place if near else source, comp].astype(jnp.float32)
                table[pl.ds(place * (owned * PAD) + comp, owned, stride=PAD), :] = values

    @pl.when(step >= fill_steps)
    def _():
        first = (step - fill_steps) * group_rows
        coef = [coef_ref[pl.ds(k, 1), :] for k in range(11)]
        ax, ay, az, tx, ty, tz, ux, uy, nh, nv, nc = coef

        def fetch(index):
            return table[pl.ds(pl.multiple_of(rows_ref[index], PAD), PAD), :]

        def close(batch):
            turned = squares[pl.ds(pl.multiple_of(batch * batch_rows, batch_rows), batch_rows), :].T
            total = jnp.sum(turned, axis=0, keepdims=True)
            sumsq_ref[0, pl.ds(batch, 1), :] = total + before_ref[0, pl.ds(batch, 1), :]

        squares[pl.ds(0, batch_rows), :] = jnp.zeros((batch_rows, LANES), jnp.float32)

        @pl.loop(0, group_rows // batch_rows)
        def _(batch):
            close(jnp.maximum(batch - 1, 0))
            base = first + batch * batch_rows
            for j in range(batch_rows):
                i = base + j
                picked[pl.ds(j * PAD, PAD), :] = fetch(i) - fetch(total_rows + i)
                picked[pl.ds((batch_rows + j) * PAD, PAD), :] = fetch(2 * total_rows + i) - fetch(3 * total_rows + i)
            for g in range(UNROLL):
                start = g * SUBLANES
                sx, sy, sz = (picked[pl.ds(start * PAD + k, SUBLANES, stride=PAD), :] for k in range(3))
                rx, ry, rz = (picked[pl.ds((batch_rows + start) * PAD + k, SUBLANES, stride=PAD), :] for k in range(3))
                sn = sx * ax + sy * ay + sz * az
                rn = rx * ax + ry * ay + rz * az
                st = sx * tx + sy * ty + sz * tz
                rt = rx * tx + ry * ty + rz * tz
                sp = sx * ux + sy * uy
                rp = rx * ux + ry * uy
                dot = sx * rx + sy * ry + sz * rz
                both = sn * rn
                values = (nh * (dot - both), nv * both, nc * (st * rn + sn * rt), nc * (sp * rn + sn * rp))
                place = ((base if near else batch * batch_rows) + start) * 4
                for k in range(4):
                    sens_ref[pl.ds(place + k, SUBLANES, stride=4), :] = values[k]
                squares[pl.ds(batch * batch_rows + start, SUBLANES), :] = (
                    values[0] * values[0] + values[1] * values[1] + values[2] * values[2] + values[3] * values[3]
                )

        close(group_rows // batch_rows - 1)


def sens_block(rows, fields, pool, lane_block, cell_block, coef, before, near, fill_steps, group_rows):
    shards, comps, owned, _ = fields.shape
    total = rows.size // 4
    groups = total // group_rows
    if near:
        fields_spec = sens_spec = pl.BlockSpec(memory_space=pltpu.VMEM)
        sens_shape = pltpu.VMEM((total * 4, LANES), jnp.float32)
    else:
        sens_spec = pl.BlockSpec((group_rows * 4, LANES), lambda i: (jnp.maximum(i - fill_steps, 0), 0))
        sens_shape = pltpu.HBM((total * 4, LANES), jnp.float32)
        fields_spec = pl.BlockSpec(
            (shards // fill_steps, comps, owned, LANES), lambda i: (jnp.minimum(i, fill_steps - 1), 0, 0, lane_block)
        )
    sums = pl.BlockSpec((1, group_rows // LANES, LANES), lambda i: (jnp.maximum(i - fill_steps, 0), 0, 0))
    pools = [] if pool is None else [pool]
    pool_rows = sum(p.shape[1] for p in pools)
    return pl.pallas_call(
        functools.partial(sens_kernel, shards // fill_steps, fill_steps, group_rows, near),
        grid=(fill_steps + groups,),
        in_specs=[
            pl.BlockSpec(memory_space=pl.ANY),
            fields_spec,
            pl.BlockSpec((16, LANES), lambda i: (0, 0)),
            sums,
        ]
        + [pl.BlockSpec((comps, pool_rows, LANES), lambda i: (0, 0, cell_block)) for _ in pools],
        out_specs=[sens_spec, sums],
        out_shape=[
            sens_shape,
            jax.ShapeDtypeStruct((groups, group_rows // LANES, LANES), jnp.float32),
        ],
        scratch_shapes=[
            pltpu.VMEM(((shards * owned + pool_rows) * PAD, LANES), jnp.float32),
            pltpu.VMEM((2 * UNROLL * SUBLANES * PAD, LANES), jnp.float32),
            pltpu.VMEM((group_rows, LANES), jnp.float32),
            pltpu.SMEM(rows.shape, jnp.int32),
            pltpu.SemaphoreType.DMA,
        ],
        cost_estimate=pl.CostEstimate(
            flops=total * LANES * 64,
            bytes_accessed=(shards * comps * owned * LANES * 2 + total * 5 * LANES * 4) * 4,
            transcendentals=0,
        ),
        compiler_params=pltpu.CompilerParams(vmem_limit_bytes=SENS_LIMIT),
        name="sens_block",
    )(rows, fields, coef, before, *pools)


def scale_kernel(inverse, far, mine_ref, theirs_ref, *refs):
    sens_refs, (out_ref, cover_ref, held, ready, spread, cover, in_sems, out_sems) = refs[:-8], refs[-8:]
    far_refs, near_refs = sens_refs[:far], sens_refs[far:]
    rows = spread.shape[0]
    step_rows = rows // 4
    steps = ready.shape[0] // step_rows

    def arrive(step, b):
        part = pl.ds(pl.multiple_of(step * rows, rows), rows)
        return pltpu.make_async_copy(far_refs[b].at[part], held.at[b, part], in_sems.at[step, b])

    def leave(step):
        part = pl.ds(pl.multiple_of(step * step_rows, step_rows), step_rows)
        return pltpu.make_async_copy(ready.at[part], out_ref.at[part], out_sems.at[step])

    for step in range(steps):
        for b in range(far):
            arrive(step, b).start()
    cover[...] = jnp.zeros_like(cover)

    @pl.loop(0, steps)
    def _(step):
        for k in range(step_rows // LANES):
            line = pl.ds(step * (step_rows // LANES) + k, 1)
            meansq = (mine_ref[line, :] + theirs_ref[line, :]) * inverse
            column = jnp.broadcast_to(lax.rsqrt(meansq + 1e-06), (LANES, LANES)).T
            for p in range(4):
                spread[pl.ds(k * 4 * LANES + p, LANES, stride=4), :] = column
        part = pl.ds(pl.multiple_of(step * rows, rows), rows)

        def write(b, values):
            normed = values * spread[...]
            place = pl.ds(pl.multiple_of(step * step_rows, step_rows), step_rows)
            lanes = slice(b * LANES, (b + 1) * LANES)
            ready[place, :, lanes] = normed.astype(ready.dtype).reshape(step_rows, 4, LANES)
            squares = (normed * normed).reshape(rows // SUBLANES, SUBLANES, LANES)
            cover[pl.ds(b * SUBLANES, SUBLANES), :] += jnp.sum(squares, axis=0)

        for b, ref in enumerate(near_refs):
            write(far + b, ref[part, :])
        for b in range(far):
            arrive(step, b).wait()
            write(b, held[b, part, :])
        leave(step).start()

    for b in range(len(sens_refs)):
        cover_ref[pl.ds(b, 1), :] = jnp.sum(cover[pl.ds(b * SUBLANES, SUBLANES), :], axis=0, keepdims=True)
    for step in range(steps):
        leave(step).wait()


def scaled(mine, theirs, inverse, far, near, step_rows):
    columns, total = len(far) + len(near), (far + near)[0].shape[0] // 4
    steps = total // step_rows
    near = [pltpu.with_memory_space_constraint(s, pltpu.VMEM) for s in near]
    whole = pl.BlockSpec(memory_space=pltpu.VMEM)
    out, cover = pl.pallas_call(
        functools.partial(scale_kernel, inverse, len(far)),
        in_specs=[whole, whole] + [pl.BlockSpec(memory_space=pltpu.HBM)] * len(far) + [whole] * len(near),
        out_specs=[pl.BlockSpec(memory_space=pltpu.HBM), whole],
        out_shape=[
            jax.ShapeDtypeStruct((total, 4, columns * LANES), jnp.bfloat16),
            jax.ShapeDtypeStruct((columns, LANES), jnp.float32),
        ],
        scratch_shapes=[
            pltpu.VMEM((len(far), total * 4, LANES), jnp.float32),
            pltpu.VMEM((total, 4, columns * LANES), jnp.bfloat16),
            pltpu.VMEM((step_rows * 4, LANES), jnp.float32),
            pltpu.VMEM((columns * SUBLANES, LANES), jnp.float32),
            pltpu.SemaphoreType.DMA((steps, len(far))),
            pltpu.SemaphoreType.DMA((steps,)),
        ],
        compiler_params=pltpu.CompilerParams(vmem_limit_bytes=SCALE_LIMIT),
        name="scaled",
    )(mine.reshape(-1, LANES), theirs.reshape(-1, LANES), *far, *near)
    return out, cover.reshape(columns * LANES)


def sum_over_cells(x, shards):
    if shards & (shards - 1):
        return lax.psum(x, "cell"), jnp.zeros_like(x)
    other, bit = jnp.zeros_like(x), 1
    while bit < shards:
        x = x + other
        other = lax.ppermute(x, "cell", [(i, i ^ bit) for i in range(shards)])
        bit *= 2
    return x, other


def coefficients(horiz, vertical, tilt_angle, azimuth):
    sin_t, cos_t = jnp.sin(tilt_angle), jnp.cos(tilt_angle)
    sin_p, cos_p = jnp.sin(azimuth), jnp.cos(azimuth)
    zero = jnp.zeros_like(horiz)
    return jnp.stack(
        [
            sin_t * cos_p,
            sin_t * sin_p,
            cos_t,
            cos_t * cos_p,
            cos_t * sin_p,
            -sin_t,
            -sin_t * sin_p,
            sin_t * cos_p,
            -horiz,
            -vertical,
            horiz - vertical,
        ]
        + [zero] * 5
    )


def scatter_over_cells(x, shards):
    if shards & (shards - 1):
        return lax.psum_scatter(x, "cell", scatter_dimension=0, tiled=False)
    me, bit = lax.axis_index("cell"), 1
    while bit < shards:
        x = x.reshape((x.shape[0] // 2, 2) + x.shape[1:])
        own = (me // bit) % 2
        kept, sent = (lax.dynamic_index_in_dim(x, k, axis=1, keepdims=False) for k in (own, 1 - own))
        x = kept + lax.ppermute(sent, "cell", [(i, i ^ bit) for i in range(shards)])
        bit *= 2
    return x[0]


def cell_parts(fields, shards):
    cell_dev = fields.shape[2] // shards
    if fields.size * fields.dtype.itemsize <= 16 * MIB:
        return (cell_dev - LANES, LANES)
    return (LANES,) * (cell_dev // LANES)


def transfer_and_solve(ready, fields, quads, tables, properties, kept, pool_rows, shards):
    comps, owned, cells = fields.shape
    cell_dev = cells // shards
    total = quads.shape[1]
    coef = coefficients(*properties)
    rank, slot, place = tables or (None, None, None)
    rows = quads * PAD if rank is None else table_rows(quads, place)
    pool = None
    if pool_rows:
        pool = scatter_over_cells(send_order(fields, slot, pool_rows, shards, 0, cell_dev), shards)
    rows = rows.reshape(-1)
    far, near, before = [], [], jnp.zeros((total // GROUP_ROWS, GROUP_ROWS // LANES, LANES), jnp.float32)

    def finish(received, first, before, last):
        width = received.shape[-1]
        here = last and width == LANES and total * 4 * LANES * 4 <= NEAR_BYTES
        for k in range(width // LANES):
            own = coef[:, first + k * LANES : first + (k + 1) * LANES]
            fill_steps, group_rows = (1, total) if here else (FILL_STEPS, GROUP_ROWS)
            before = before.reshape(total // group_rows, group_rows // LANES, LANES)
            block = first // LANES + k
            values, before = sens_block(
                rows, received, pool, k, block, own, before, here, fill_steps, group_rows
            )
            (near if here else far).append(values)
        return before

    first, received = 0, None
    for width in cell_parts(fields, shards):
        if ready is None:
            ready = send_order(fields, rank, kept, shards, first, width)
        if received is not None:
            ready, received, pool, rows, coef = lax.optimization_barrier((ready, received, pool, rows, coef))
        arriving = lax.all_to_all(ready, "cell", split_axis=0, concat_axis=0, tiled=True)
        if received is not None:
            before = finish(received, first - received.shape[-1], before, False)
        received, ready = arriving, None
        first += width
    before = finish(received, first - received.shape[-1], before, True)
    mine, theirs = sum_over_cells(before, shards)
    return scaled(mine, theirs, 1.0 / (4.0 * cell_dev * shards), far, near, SCALE_ROWS)


def local(fields, horiz, vertical, tilt_angle, azimuth, electrode_quads):
    shards = lax.axis_size("cell")
    owned = fields.shape[0]
    fields = fields.transpose(1, 0, 2)
    quads = electrode_quads.T
    properties = (horiz, vertical, tilt_angle, azimuth)
    if owned % LANES or owned > 2 * LANES:
        return transfer_and_solve(None, fields, quads, None, properties, owned, 0, shards)
    keeps = tuple(owned * part // 32 // ROW_TILE * ROW_TILE for part in KEEPS)
    pool = owned * POOL // 32 // ROW_TILE * ROW_TILE
    ready, tables, chosen = send_first(fields, quads, keeps, pool, shards, cell_parts(fields, shards)[0])

    def branch(k):
        if k == len(keeps):
            return lambda ready, tables, fields, quads, *properties: transfer_and_solve(
                None, fields, quads, None, properties, owned, 0, shards
            )
        return lambda ready, tables, fields, quads, *properties: transfer_and_solve(
            ready[k], fields, quads, tables, properties, keeps[k], 0 if k else pool, shards
        )

    branches = [branch(k) for k in range(len(keeps) + 1)]
    return lax.switch(chosen, branches, ready, tables, fields, quads, *properties)


def solution(mesh):
    placed = (
        P(("grp", "cell"), None, None),
        P(("grp", "cell")),
        P(("grp", "cell")),
        P(("grp", "cell")),
        P(("grp", "cell")),
        P("grp", None),
    )
    return jax.shard_map(
        local,
        mesh=mesh,
        in_specs=placed,
        out_specs=(P("grp", None, "cell"), P(("grp", "cell"))),
        check_vma=False,
    )
```

profile of v0, /device:TPU:0, one launch (start us, length us, event | category | flops | bytes accessed | tf_op | source)
XLA Modules:
  0.0 301.1 jit_solution(14400087371100488177)
XLA Ops:
  0.6 0.0 copy-start
  0.6 0.0 copy-start.1
  0.7 0.0 copy-start.2
  0.7 0.0 copy-start.3
  0.7 0.0 copy-start.4
  0.7 9.4 %send_first.1 = (bf16[16,3,224,384]{3,2,1,0:T(8,128)(2,1)}, bf16[16,3,240,384]{3,2,1,0:T(8,128)(2,1)}, f32[32,128]{1,0:T(8,128)S(1)}, f32[32,128]{1,0:T(8,128)S(1)}, f32[32,128]{1,0:T(8,128)S(1)}, /*index=5*/s32[1]{0:T(128)}) custom-call(bf16[3,256,8192]{2,1,0:T(8,128)(2,1)} %bitcast.90, s32[4,2048]{1,0:T(4,128)} %bitcast.100), custom_call_target="tpu_custom_call" | custom-call | tf_op jit(solution)/shard_map/send_first/pallas_call | solution.py:187
  10.8 0.0 copy-done
  10.8 0.0 copy-done.1
  10.8 0.0 copy-done.2
  10.8 0.0 copy-done.3
  10.8 0.0 copy-done.4
  10.8 290.1 %conditional.1 = (bf16[2048,4,512]{2,1,0:T(4,128)(2,1)}, f32[512]{0:T(512)}) conditional(s32[]{:T(128)} %bitcast.54, (bf16[3,256,8192]{2,1,0:T(8,128)(2,1)}, f32[32,128]{1,0:T(8,128)S(1)}, bf16[16,3,224,384]{3,2,1,0:T(8,128)(2,1)}, f32[32,128]{1,0:T(8,128)S(1)}, s32[4,2048]{1,0:T(4,128)S(1)}, /*index=5*/f32[32,128]{1,0:T(8,128)S(1)}, ...), branch_computations={%region_0.1_spmd, %region_1.2_spmd, %region_2.3_spmd} | conditional | flops 68041320 | bytes 209466832 | solution.py:551
  10.8 7.4 %all-to-all-start = ((bf16[16,3,224,384]{3,2,1,0:T(8,128)(2,1)}), bf16[16,3,224,384]{3,2,1,0:T(8,128)(2,1)}, u32[]{:S(2)}, u32[]{:S(2)}) async-start(bf16[16,3,224,384]{3,2,1,0:T(8,128)(2,1)} %get-tuple-element.52), calls=%async_computation | async-start | bytes 16515072 | tf_op jit(solution)/shard_map/cond/branch_0_fun/all_to_all | solution.py:519
  18.3 6.3 %send_order.6 = bf16[16,3,40,512]{3,2,1,0:T(8,128)(2,1)} custom-call(bf16[3,256,8192]{2,1,0:T(8,128)(2,1)} %get-tuple-element.50.fields_ref, f32[32,128]{1,0:T(8,128)S(1)} %get-tuple-element.53.rank_ref), custom_call_target="tpu_custom_call" | custom-call | bytes 25165824 | tf_op jit(solution)/shard_map/cond/branch_0_fun/send_order/pallas_call | solution.py:217
  24.7 1.3 dynamic-slice_bitcast_fusion
  26.0 0.4 collective-permute-start
  26.4 2.2 collective-permute-done
  28.6 1.3 bitcast_add_fusion
  29.9 1.9 collective-permute-start.1
  31.9 45.3 %collective-permute-done.1 = bf16[4,3,40,512]{3,2,1,0:T(8,128)(2,1)S(1)} collective-permute-done((bf16[4,3,40,512]{3,2,1,0:T(8,128)(2,1)S(1)}, bf16[4,3,40,512]{3,2,1,0:T(8,128)(2,1)S(1)}, u32[]{:S(2)}, u32[]{:S(2)}) %collective-permute-start.1) | collective-permute-done | bytes 491552 | tf_op jit(solution)/shard_map/cond/branch_0_fun/ppermute | solution.py:474
  77.2 0.1 bitcast_add_fusion.1
  77.2 0.1 collective-permute-start.2
  77.4 2.1 table_rows.2
  79.5 0.8 copy.11
  80.3 5.7 %send_order.5 = bf16[16,3,224,128]{3,2,1,0:T(8,128)(2,1)} custom-call(bf16[3,256,8192]{2,1,0:T(8,128)(2,1)} %get-tuple-element.50.fields_ref, f32[32,128]{1,0:T(8,128)S(1)} %get-tuple-element.51.rank_ref), custom_call_target="tpu_custom_call" | custom-call | bytes 6291456 | tf_op jit(solution)/shard_map/cond/branch_0_fun/send_order/pallas_call | solution.py:217
  86.0 71.4 %collective-permute-done.2 = bf16[2,3,40,512]{3,2,1,0:T(8,128)(2,1)S(1)} collective-permute-done((bf16[2,3,40,512]{3,2,1,0:T(8,128)(2,1)S(1)}, bf16[2,3,40,512]{3,2,1,0:T(8,128)(2,1)S(1)}, u32[]{:S(2)}, u32[]{:S(2)}) %collective-permute-start.2) | collective-permute-done | bytes 245792 | tf_op jit(solution)/shard_map/cond/branch_0_fun/ppermute | solution.py:474
  157.5 4.6 %collective-permute-start.3 = (bf16[1,3,40,512]{3,2,1,0:T(8,128)(2,1)S(1)}, bf16[1,3,40,512]{3,2,1,0:T(8,128)(2,1)S(1)}, u32[]{:S(2)}, u32[]{:S(2)}) collective-permute-start(bf16[1,3,40,512]{3,2,1,0:T(8,128)(2,1)S(1)} %constant_dynamic-slice_fusion), channel_id=1, source_target_pairs={{0,8},{1,9},{2,10},{3,11},{4,12},{5,13},{6,14},{7,15},{8,0},{9,1},... | collective-permute-start | bytes 368648 | tf_op jit(solution)/shard_map/cond/branch_0_fun/ppermute | solution.py:474
  162.1 0.1 stack.79
  162.2 42.5 %collective-permute-done.3 = bf16[1,3,40,512]{3,2,1,0:T(8,128)(2,1)S(1)} collective-permute-done((bf16[1,3,40,512]{3,2,1,0:T(8,128)(2,1)S(1)}, bf16[1,3,40,512]{3,2,1,0:T(8,128)(2,1)S(1)}, u32[]{:S(2)}, u32[]{:S(2)}) %collective-permute-start.3) | collective-permute-done | bytes 122912 | tf_op jit(solution)/shard_map/cond/branch_0_fun/ppermute | solution.py:474
  204.7 0.0 all-to-all-done.fields_ref
  204.7 3.7 %all-to-all-start.1 = ((bf16[16,3,224,128]{3,2,1,0:T(8,128)(2,1)}), bf16[16,3,224,128]{3,2,1,0:T(8,128)(2,1)S(1)}, u32[]{:S(2)}, u32[]{:S(2)}) async-start(bf16[16,3,224,128]{3,2,1,0:T(8,128)(2,1)} %send_order.5), calls=%async_computation.1 | async-start | bytes 5505024 | tf_op jit(solution)/shard_map/cond/branch_0_fun/all_to_all | solution.py:519
  208.5 12.2 %sens_block.12 = (f32[8192,128]{1,0:T(8,128)}, f32[4,4,128]{2,1,0:T(4,128)S(1)}) custom-call(s32[8192]{0:T(1024)S(1)} %bitcast.69, bf16[16,3,224,384]{3,2,1,0:T(8,128)(2,1)} %all-to-all-done.fields_ref, f32[16,128]{1,0:T(8,128)S(1)} %get-tuple-element.133.coef_ref, f32[4,4,128]{2,1,0:T(4,128)S(1)} %broadcast_3_before_ref.0.before_ref, ...), custom_call_target="tpu_custom_call" | custom-call | flops 16777216 | bytes 31981568 | tf_op jit(solution)/shard_map/cond/branch_0_fun/sens_block/pallas_call | solution.py:323
  220.6 12.1 %sens_block.13 = (f32[8192,128]{1,0:T(8,128)}, f32[4,4,128]{2,1,0:T(4,128)S(1)}) custom-call(s32[8192]{0:T(1024)S(1)} %bitcast.70, bf16[16,3,224,384]{3,2,1,0:T(8,128)(2,1)} %all-to-all-done.fields_ref, f32[16,128]{1,0:T(8,128)S(1)} %get-tuple-element.134.coef_ref, f32[4,4,128]{2,1,0:T(4,128)S(1)} %get-tuple-element.65.before_ref, ...), custom_call_target="tpu_custom_call" | custom-call | flops 16777216 | bytes 31981568 | tf_op jit(solution)/shard_map/cond/branch_0_fun/sens_block/pallas_call | solution.py:323
  232.7 12.1 %sens_block.14 = (f32[8192,128]{1,0:T(8,128)}, f32[4,4,128]{2,1,0:T(4,128)S(1)}) custom-call(s32[8192]{0:T(1024)S(1)} %bitcast.71, bf16[16,3,224,384]{3,2,1,0:T(8,128)(2,1)} %all-to-all-done.fields_ref, f32[16,128]{1,0:T(8,128)S(1)} %get-tuple-element.135.coef_ref, f32[4,4,128]{2,1,0:T(4,128)S(1)} %get-tuple-element.66.before_ref, ...), custom_call_target="tpu_custom_call" | custom-call | flops 16777216 | bytes 31981568 | tf_op jit(solution)/shard_map/cond/branch_0_fun/sens_block/pallas_call | solution.py:323
  244.8 16.1 %all-to-all-done.1.fields_ref = bf16[16,3,224,128]{3,2,1,0:T(8,128)(2,1)S(1)} async-done(((bf16[16,3,224,128]{3,2,1,0:T(8,128)(2,1)}), bf16[16,3,224,128]{3,2,1,0:T(8,128)(2,1)S(1)}, u32[]{:S(2)}, u32[]{:S(2)}) %all-to-all-start.1) | async-done | bytes 2752544 | tf_op jit(solution)/shard_map/cond/branch_0_fun/all_to_all | solution.py:519
  260.9 8.9 %sens_block.15 = (f32[8192,128]{1,0:T(8,128)S(1)}, f32[1,16,128]{2,1,0:T(8,128)S(1)}) custom-call(s32[8192]{0:T(1024)S(1)} %bitcast.72, bf16[16,3,224,128]{3,2,1,0:T(8,128)(2,1)S(1)} %all-to-all-done.1.fields_ref, f32[16,128]{1,0:T(8,128)S(1)} %get-tuple-element.136.coef_ref, f32[1,16,128]{2,1,0:T(8,128)S(1)} %bitcast.87, ...), custom_call_target="tpu_custom_call" | custom-call | flops 16777216 | bytes 31981568 | tf_op jit(solution)/shard_map/cond/branch_0_fun/sens_block/pallas_call | solution.py:323
  269.8 0.8 collective-permute-start.4
  270.6 0.8 collective-permute-done.4
  271.4 4.2 %collective-permute-start.5 = (f32[1,16,128]{2,1,0:T(8,128)S(1)}, f32[1,16,128]{2,1,0:T(8,128)S(1)}, u32[]{:S(2)}, u32[]{:S(2)}) collective-permute-start(f32[1,16,128]{2,1,0:T(8,128)S(1)} %add.79), channel_id=1, source_target_pairs={{0,2},{1,3},{2,0},{3,1},{4,6},{5,7},{6,4},{7,5},{8,10},{9,11},{10,... | collective-permute-start | bytes 24584 | tf_op jit(solution)/shard_map/cond/branch_0_fun/ppermute | solution.py:439
  275.7 1.6 collective-permute-done.5
  277.3 7.5 %collective-permute-start.6 = (f32[1,16,128]{2,1,0:T(8,128)S(1)}, f32[1,16,128]{2,1,0:T(8,128)S(1)}, u32[]{:S(2)}, u32[]{:S(2)}) collective-permute-start(f32[1,16,128]{2,1,0:T(8,128)S(1)} %add.80), channel_id=1, source_target_pairs={{0,4},{1,5},{2,6},{3,7},{4,0},{5,1},{6,2},{7,3},{8,12},{9,13},{10,... | collective-permute-start | bytes 24584 | tf_op jit(solution)/shard_map/cond/branch_0_fun/ppermute | solution.py:439
  284.8 1.6 collective-permute-done.6
  286.5 3.9 %collective-permute-start.7 = (f32[1,16,128]{2,1,0:T(8,128)S(1)}, f32[1,16,128]{2,1,0:T(8,128)S(1)}, u32[]{:S(2)}, u32[]{:S(2)}) collective-permute-start(f32[1,16,128]{2,1,0:T(8,128)S(1)} %add.81), channel_id=1, source_target_pairs={{0,8},{1,9},{2,10},{3,11},{4,12},{5,13},{6,14},{7,15},{8,0},{9,1},... | collective-permute-start | bytes 24584 | tf_op jit(solution)/shard_map/cond/branch_0_fun/ppermute | solution.py:439
  290.3 1.6 collective-permute-done.7
  292.0 8.7 %scaled.3 = (bf16[2048,4,512]{2,1,0:T(4,128)(2,1)}, f32[4,128]{1,0:T(4,128)}) custom-call(f32[16,128]{1,0:T(8,128)S(1)} %bitcast.81, f32[16,128]{1,0:T(8,128)S(1)} %bitcast.84, f32[8192,128]{1,0:T(8,128)} %get-tuple-element.69.refs_0_, f32[8192,128]{1,0:T(8,128)} %get-tuple-element.70.refs_1_, f32[8192,128]{1,0:T(8,128)} %get-tuple-element.71.refs_2_, ...), custom_call_target="tpu_custom_call" | custom-call | tf_op jit(solution)/shard_map/cond/branch_0_fun/scaled/pallas_call | solution.py:411
  (15 shorter events, 0.2 us)
Async XLA Ops:
  0.6 10.2 %copy-start = (s32[2048,4]{0,1:T(4,128)S(1)}, s32[2048,4]{0,1:T(4,128)}, u32[]{:S(2)}) copy-start(s32[2048,4]{0,1:T(4,128)} %param.14) | copy-start | bytes 98308
  0.6 10.2 %copy-start.1 = (f32[512]{0:T(512)S(1)}, f32[512]{0:T(512)}, u32[]{:S(2)}) copy-start(f32[512]{0:T(512)} %param.13) | copy-start | bytes 6148
  0.7 10.2 %copy-start.2 = (f32[512]{0:T(512)S(1)}, f32[512]{0:T(512)}, u32[]{:S(2)}) copy-start(f32[512]{0:T(512)} %param.12) | copy-start | bytes 6148
  0.7 10.2 %copy-start.3 = (f32[512]{0:T(512)S(1)}, f32[512]{0:T(512)}, u32[]{:S(2)}) copy-start(f32[512]{0:T(512)} %param.10) | copy-start | bytes 6148
  0.7 10.2 %copy-start.4 = (f32[512]{0:T(512)S(1)}, f32[512]{0:T(512)}, u32[]{:S(2)}) copy-start(f32[512]{0:T(512)} %param.11) | copy-start | bytes 6148
  10.8 193.8 %all-to-all-start = ((bf16[16,3,224,384]{3,2,1,0:T(8,128)(2,1)}), bf16[16,3,224,384]{3,2,1,0:T(8,128)(2,1)}, u32[]{:S(2)}, u32[]{:S(2)}) async-start(bf16[16,3,224,384]{3,2,1,0:T(8,128)(2,1)} %get-tuple-element.52), calls=%async_computation | async-start | bytes 16515072 | tf_op jit(solution)/shard_map/cond/branch_0_fun/all_to_all | solution.py:519
  26.0 2.6 collective-permute-start
  29.9 47.2 %collective-permute-start.1 = (bf16[4,3,40,512]{3,2,1,0:T(8,128)(2,1)S(1)}, bf16[4,3,40,512]{3,2,1,0:T(8,128)(2,1)S(1)}, u32[]{:S(2)}, u32[]{:S(2)}) collective-permute-start(bf16[4,3,40,512]{3,2,1,0:T(8,128)(2,1)S(1)} %dynamic-slice_bitcast_fusion.1), channel_id=1, source_target_pairs={{0,2},{1,3},{2,0},{3,1},{4,6},{5,7},{6,4},{7,5},{8,10},{9,11},{10,... | collective-permute-start | bytes 1474568 | tf_op jit(solution)/shard_map/cond/branch_0_fun/ppermute | solution.py:474
  77.2 80.2 %collective-permute-start.2 = (bf16[2,3,40,512]{3,2,1,0:T(8,128)(2,1)S(1)}, bf16[2,3,40,512]{3,2,1,0:T(8,128)(2,1)S(1)}, u32[]{:S(2)}, u32[]{:S(2)}) collective-permute-start(bf16[2,3,40,512]{3,2,1,0:T(8,128)(2,1)S(1)} %dynamic-slice_bitcast_fusion.2), channel_id=1, source_target_pairs={{0,4},{1,5},{2,6},{3,7},{4,0},{5,1},{6,2},{7,3},{8,12},{9,13},{10,... | collective-permute-start | bytes 737288 | tf_op jit(solution)/shard_map/cond/branch_0_fun/ppermute | solution.py:474
  157.5 47.1 %collective-permute-start.3 = (bf16[1,3,40,512]{3,2,1,0:T(8,128)(2,1)S(1)}, bf16[1,3,40,512]{3,2,1,0:T(8,128)(2,1)S(1)}, u32[]{:S(2)}, u32[]{:S(2)}) collective-permute-start(bf16[1,3,40,512]{3,2,1,0:T(8,128)(2,1)S(1)} %constant_dynamic-slice_fusion), channel_id=1, source_target_pairs={{0,8},{1,9},{2,10},{3,11},{4,12},{5,13},{6,14},{7,15},{8,0},{9,1},... | collective-permute-start | bytes 368648 | tf_op jit(solution)/shard_map/cond/branch_0_fun/ppermute | solution.py:474
  204.7 56.2 %all-to-all-start.1 = ((bf16[16,3,224,128]{3,2,1,0:T(8,128)(2,1)}), bf16[16,3,224,128]{3,2,1,0:T(8,128)(2,1)S(1)}, u32[]{:S(2)}, u32[]{:S(2)}) async-start(bf16[16,3,224,128]{3,2,1,0:T(8,128)(2,1)} %send_order.5), calls=%async_computation.1 | async-start | bytes 5505024 | tf_op jit(solution)/shard_map/cond/branch_0_fun/all_to_all | solution.py:519
  269.8 1.7 collective-permute-start.4
  271.4 5.9 %collective-permute-start.5 = (f32[1,16,128]{2,1,0:T(8,128)S(1)}, f32[1,16,128]{2,1,0:T(8,128)S(1)}, u32[]{:S(2)}, u32[]{:S(2)}) collective-permute-start(f32[1,16,128]{2,1,0:T(8,128)S(1)} %add.79), channel_id=1, source_target_pairs={{0,2},{1,3},{2,0},{3,1},{4,6},{5,7},{6,4},{7,5},{8,10},{9,11},{10,... | collective-permute-start | bytes 24584 | tf_op jit(solution)/shard_map/cond/branch_0_fun/ppermute | solution.py:439
  277.3 9.1 %collective-permute-start.6 = (f32[1,16,128]{2,1,0:T(8,128)S(1)}, f32[1,16,128]{2,1,0:T(8,128)S(1)}, u32[]{:S(2)}, u32[]{:S(2)}) collective-permute-start(f32[1,16,128]{2,1,0:T(8,128)S(1)} %add.80), channel_id=1, source_target_pairs={{0,4},{1,5},{2,6},{3,7},{4,0},{5,1},{6,2},{7,3},{8,12},{9,13},{10,... | collective-permute-start | bytes 24584 | tf_op jit(solution)/shard_map/cond/branch_0_fun/ppermute | solution.py:439
  286.5 5.5 %collective-permute-start.7 = (f32[1,16,128]{2,1,0:T(8,128)S(1)}, f32[1,16,128]{2,1,0:T(8,128)S(1)}, u32[]{:S(2)}, u32[]{:S(2)}) collective-permute-start(f32[1,16,128]{2,1,0:T(8,128)S(1)} %add.81), channel_id=1, source_target_pairs={{0,8},{1,9},{2,10},{3,11},{4,12},{5,13},{6,14},{7,15},{8,0},{9,1},... | collective-permute-start | bytes 24584 | tf_op jit(solution)/shard_map/cond/branch_0_fun/ppermute | solution.py:439
where the time goes:
time: 302 us; the launch traced here: 301 us
  waiting for transfers between devices  183 us (61%)
  Pallas kernels  77.5 us (26%)
  starting transfers between devices  34.6 us (11%)
    ppermute x4, waiting for transfers between devices, scatter_over_cells(): x = kept + lax.ppermute(sent, 'cell', [(i, i ^ bit) for i in range(shards)])  161 us
    pallas_call x4, Pallas kernels, sens_block(): pl.pallas_call(functools.partial(sens_kernel, shards // fill_steps, fill_...  45.2 us
    ppermute x4, starting transfers between devices, sum_over_cells(): other = lax.ppermute(x, 'cell', [(i, i ^ bit) for i in range(shards)])  16.5 us
    all_to_all x2, waiting for transfers between devices, transfer_and_solve(): lax.all_to_all(ready, 'cell', split_axis=0, concat_axis=0, tiled=True)  16.1 us
    pallas_call x2, Pallas kernels, send_order(): pl.pallas_call(functools.partial(send_order_kernel if rank is None else s...  12 us
    all_to_all x2, starting transfers between devices, transfer_and_solve(): lax.all_to_all(ready, 'cell', split_axis=0, concat_axis=0, tiled=True)  11.2 us
    pallas_call x1, Pallas kernels, send_first(): pl.pallas_call(functools.partial(send_first_kernel, keeps, pool), in_spec...  9.45 us
    pallas_call x1, Pallas kernels, scaled(): pl.pallas_call(functools.partial(scale_kernel, inverse, len(far)), in_spe...  8.71 us
  transfers between devices with their start and end apart: 10, of which 9 were waited for; matrix products, arithmetic and copies ran while one was open for 1% of the time, Pallas kernels for 17%

commit v1 on v0

--- a/solution.py
+++ b/solution.py
@@ -433,11 +433,12 @@
 def sum_over_cells(x, shards):
     if shards & (shards - 1):
         return lax.psum(x, "cell"), jnp.zeros_like(x)
-    other, bit = jnp.zeros_like(x), 1
-    while bit < shards:
+    other, unit = jnp.zeros_like(x), 1
+    while unit < shards:
         x = x + other
-        other = lax.ppermute(x, "cell", [(i, i ^ bit) for i in range(shards)])
-        bit *= 2
+        size = 4 if unit in (4,) and unit * 4 <= shards else 2
+        other = sum(lax.ppermute(x, "cell", [(i, i ^ (k * unit)) for i in range(shards)]) for k in range(1, size))
+        unit *= size
     return x, other
 
 

time: 302 us -> 300 us (level)
    ppermute x4 -> x5, starting transfers between devices: 16.5 us -> 15 us  [sum_over_cells(): lax.ppermute(x, 'cell', [(i, i ^ k * unit) for i in range(shards)])]
  transfers between devices with their start and end apart: 10 -> 11, of which waited for: 9 -> 10; matrix products, arithmetic and copies ran while one was open for 1% -> 1% of each run, Pallas kernels for 17% -> 17%
where the time goes in v1:
time: 300 us; the launch traced here: 299 us
  waiting for transfers between devices  183 us (61%)
  Pallas kernels  77.4 us (26%)
  starting transfers between devices  33.1 us (11%)
    ppermute x4, waiting for transfers between devices, scatter_over_cells(): x = kept + lax.ppermute(sent, 'cell', [(i, i ^ bit) for i in range(shards)])  161 us
    pallas_call x4, Pallas kernels, sens_block(): pl.pallas_call(functools.partial(sens_kernel, shards // fill_steps, fill_...  45.1 us
    all_to_all x2, waiting for transfers between devices, transfer_and_solve(): lax.all_to_all(ready, 'cell', split_axis=0, concat_axis=0, tiled=True)  16.1 us
    ppermute x5, starting transfers between devices, sum_over_cells(): lax.ppermute(x, 'cell', [(i, i ^ k * unit) for i in range(shards)])  15 us
    pallas_call x2, Pallas kernels, send_order(): pl.pallas_call(functools.partial(send_order_kernel if rank is None else s...  12 us
    all_to_all x2, starting transfers between devices, transfer_and_solve(): lax.all_to_all(ready, 'cell', split_axis=0, concat_axis=0, tiled=True)  11.2 us
    pallas_call x1, Pallas kernels, send_first(): pl.pallas_call(functools.partial(send_first_kernel, keeps, pool), in_spec...  9.45 us
    pallas_call x1, Pallas kernels, scaled(): pl.pallas_call(functools.partial(scale_kernel, inverse, len(far)), in_spe...  8.71 us
  transfers between devices with their start and end apart: 11, of which 10 were waited for; matrix products, arithmetic and copies ran while one was open for 1% of the time, Pallas kernels for 17%

profile of v1, /device:TPU:0, one launch (start us, length us, event | category | flops | bytes accessed | tf_op | source)
XLA Modules:
  0.0 299.4 jit_solution(5778715283958689287)
XLA Ops:
  0.6 0.0 copy-start
  0.6 0.0 copy-start.1
  0.7 0.0 copy-start.2
  0.7 0.0 copy-start.3
  0.7 0.0 copy-start.4
  0.7 9.4 %send_first.1 = (bf16[16,3,224,384]{3,2,1,0:T(8,128)(2,1)}, bf16[16,3,240,384]{3,2,1,0:T(8,128)(2,1)}, f32[32,128]{1,0:T(8,128)S(1)}, f32[32,128]{1,0:T(8,128)S(1)}, f32[32,128]{1,0:T(8,128)S(1)}, /*index=5*/s32[1]{0:T(128)}) custom-call(bf16[3,256,8192]{2,1,0:T(8,128)(2,1)} %bitcast.90, s32[4,2048]{1,0:T(4,128)} %bitcast.100), custom_call_target="tpu_custom_call" | custom-call | tf_op jit(solution)/shard_map/send_first/pallas_call | solution.py:187
  10.8 0.0 copy-done
  10.8 0.0 copy-done.1
  10.8 0.0 copy-done.2
  10.8 0.0 copy-done.3
  10.8 0.0 copy-done.4
  10.8 288.4 %conditional.1 = (bf16[2048,4,512]{2,1,0:T(4,128)(2,1)}, f32[512]{0:T(512)}) conditional(s32[]{:T(128)} %bitcast.54, (bf16[3,256,8192]{2,1,0:T(8,128)(2,1)}, f32[32,128]{1,0:T(8,128)S(1)}, bf16[16,3,224,384]{3,2,1,0:T(8,128)(2,1)}, f32[32,128]{1,0:T(8,128)S(1)}, s32[4,2048]{1,0:T(4,128)S(1)}, /*index=5*/f32[32,128]{1,0:T(8,128)S(1)}, ...), branch_computations={%region_0.1_spmd, %region_1.2_spmd, %region_2.3_spmd} | conditional | flops 68043368 | bytes 209507824 | solution.py:552
  10.8 7.4 %all-to-all-start = ((bf16[16,3,224,384]{3,2,1,0:T(8,128)(2,1)}), bf16[16,3,224,384]{3,2,1,0:T(8,128)(2,1)}, u32[]{:S(2)}, u32[]{:S(2)}) async-start(bf16[16,3,224,384]{3,2,1,0:T(8,128)(2,1)} %get-tuple-element.52), calls=%async_computation | async-start | bytes 16515072 | tf_op jit(solution)/shard_map/cond/branch_0_fun/all_to_all | solution.py:520
  18.3 6.3 %send_order.6 = bf16[16,3,40,512]{3,2,1,0:T(8,128)(2,1)} custom-call(bf16[3,256,8192]{2,1,0:T(8,128)(2,1)} %get-tuple-element.50.fields_ref, f32[32,128]{1,0:T(8,128)S(1)} %get-tuple-element.53.rank_ref), custom_call_target="tpu_custom_call" | custom-call | bytes 25165824 | tf_op jit(solution)/shard_map/cond/branch_0_fun/send_order/pallas_call | solution.py:217
  24.7 1.3 dynamic-slice_bitcast_fusion
  26.0 0.4 collective-permute-start
  26.4 2.2 collective-permute-done
  28.6 1.3 bitcast_add_fusion
  29.9 1.9 collective-permute-start.1
  31.9 45.3 %collective-permute-done.1 = bf16[4,3,40,512]{3,2,1,0:T(8,128)(2,1)S(1)} collective-permute-done((bf16[4,3,40,512]{3,2,1,0:T(8,128)(2,1)S(1)}, bf16[4,3,40,512]{3,2,1,0:T(8,128)(2,1)S(1)}, u32[]{:S(2)}, u32[]{:S(2)}) %collective-permute-start.1) | collective-permute-done | bytes 491552 | tf_op jit(solution)/shard_map/cond/branch_0_fun/ppermute | solution.py:475
  77.2 0.1 bitcast_add_fusion.1
  77.2 0.1 collective-permute-start.2
  77.4 2.1 table_rows.2
  79.5 0.8 copy.11
  80.3 5.7 %send_order.5 = bf16[16,3,224,128]{3,2,1,0:T(8,128)(2,1)} custom-call(bf16[3,256,8192]{2,1,0:T(8,128)(2,1)} %get-tuple-element.50.fields_ref, f32[32,128]{1,0:T(8,128)S(1)} %get-tuple-element.51.rank_ref), custom_call_target="tpu_custom_call" | custom-call | bytes 6291456 | tf_op jit(solution)/shard_map/cond/branch_0_fun/send_order/pallas_call | solution.py:217
  86.0 71.5 %collective-permute-done.2 = bf16[2,3,40,512]{3,2,1,0:T(8,128)(2,1)S(1)} collective-permute-done((bf16[2,3,40,512]{3,2,1,0:T(8,128)(2,1)S(1)}, bf16[2,3,40,512]{3,2,1,0:T(8,128)(2,1)S(1)}, u32[]{:S(2)}, u32[]{:S(2)}) %collective-permute-start.2) | collective-permute-done | bytes 245792 | tf_op jit(solution)/shard_map/cond/branch_0_fun/ppermute | solution.py:475
  157.5 4.6 %collective-permute-start.3 = (bf16[1,3,40,512]{3,2,1,0:T(8,128)(2,1)S(1)}, bf16[1,3,40,512]{3,2,1,0:T(8,128)(2,1)S(1)}, u32[]{:S(2)}, u32[]{:S(2)}) collective-permute-start(bf16[1,3,40,512]{3,2,1,0:T(8,128)(2,1)S(1)} %constant_dynamic-slice_fusion), channel_id=1, source_target_pairs={{0,8},{1,9},{2,10},{3,11},{4,12},{5,13},{6,14},{7,15},{8,0},{9,1},... | collective-permute-start | bytes 368648 | tf_op jit(solution)/shard_map/cond/branch_0_fun/ppermute | solution.py:475
  162.1 0.1 stack.79
  162.2 42.5 %collective-permute-done.3 = bf16[1,3,40,512]{3,2,1,0:T(8,128)(2,1)S(1)} collective-permute-done((bf16[1,3,40,512]{3,2,1,0:T(8,128)(2,1)S(1)}, bf16[1,3,40,512]{3,2,1,0:T(8,128)(2,1)S(1)}, u32[]{:S(2)}, u32[]{:S(2)}) %collective-permute-start.3) | collective-permute-done | bytes 122912 | tf_op jit(solution)/shard_map/cond/branch_0_fun/ppermute | solution.py:475
  204.7 0.0 all-to-all-done.fields_ref
  204.7 3.7 %all-to-all-start.1 = ((bf16[16,3,224,128]{3,2,1,0:T(8,128)(2,1)}), bf16[16,3,224,128]{3,2,1,0:T(8,128)(2,1)S(1)}, u32[]{:S(2)}, u32[]{:S(2)}) async-start(bf16[16,3,224,128]{3,2,1,0:T(8,128)(2,1)} %send_order.5), calls=%async_computation.1 | async-start | bytes 5505024 | tf_op jit(solution)/shard_map/cond/branch_0_fun/all_to_all | solution.py:520
  208.5 12.1 %sens_block.12 = (f32[8192,128]{1,0:T(8,128)}, f32[4,4,128]{2,1,0:T(4,128)S(1)}) custom-call(s32[8192]{0:T(1024)S(1)} %bitcast.72, bf16[16,3,224,384]{3,2,1,0:T(8,128)(2,1)} %all-to-all-done.fields_ref, f32[16,128]{1,0:T(8,128)S(1)} %get-tuple-element.133.coef_ref, f32[4,4,128]{2,1,0:T(4,128)S(1)} %broadcast_3_before_ref.0.before_ref, ...), custom_call_target="tpu_custom_call" | custom-call | flops 16777216 | bytes 31981568 | tf_op jit(solution)/shard_map/cond/branch_0_fun/sens_block/pallas_call | solution.py:323
  220.6 12.1 %sens_block.13 = (f32[8192,128]{1,0:T(8,128)}, f32[4,4,128]{2,1,0:T(4,128)S(1)}) custom-call(s32[8192]{0:T(1024)S(1)} %bitcast.73, bf16[16,3,224,384]{3,2,1,0:T(8,128)(2,1)} %all-to-all-done.fields_ref, f32[16,128]{1,0:T(8,128)S(1)} %get-tuple-element.134.coef_ref, f32[4,4,128]{2,1,0:T(4,128)S(1)} %get-tuple-element.65.before_ref, ...), custom_call_target="tpu_custom_call" | custom-call | flops 16777216 | bytes 31981568 | tf_op jit(solution)/shard_map/cond/branch_0_fun/sens_block/pallas_call | solution.py:323
  232.7 12.1 %sens_block.14 = (f32[8192,128]{1,0:T(8,128)}, f32[4,4,128]{2,1,0:T(4,128)S(1)}) custom-call(s32[8192]{0:T(1024)S(1)} %bitcast.74, bf16[16,3,224,384]{3,2,1,0:T(8,128)(2,1)} %all-to-all-done.fields_ref, f32[16,128]{1,0:T(8,128)S(1)} %get-tuple-element.135.coef_ref, f32[4,4,128]{2,1,0:T(4,128)S(1)} %get-tuple-element.66.before_ref, ...), custom_call_target="tpu_custom_call" | custom-call | flops 16777216 | bytes 31981568 | tf_op jit(solution)/shard_map/cond/branch_0_fun/sens_block/pallas_call | solution.py:323
  244.7 16.1 %all-to-all-done.1.fields_ref = bf16[16,3,224,128]{3,2,1,0:T(8,128)(2,1)S(1)} async-done(((bf16[16,3,224,128]{3,2,1,0:T(8,128)(2,1)}), bf16[16,3,224,128]{3,2,1,0:T(8,128)(2,1)S(1)}, u32[]{:S(2)}, u32[]{:S(2)}) %all-to-all-start.1) | async-done | bytes 2752544 | tf_op jit(solution)/shard_map/cond/branch_0_fun/all_to_all | solution.py:520
  260.9 8.9 %sens_block.15 = (f32[8192,128]{1,0:T(8,128)S(1)}, f32[1,16,128]{2,1,0:T(8,128)S(1)}) custom-call(s32[8192]{0:T(1024)S(1)} %bitcast.75, bf16[16,3,224,128]{3,2,1,0:T(8,128)(2,1)S(1)} %all-to-all-done.1.fields_ref, f32[16,128]{1,0:T(8,128)S(1)} %get-tuple-element.136.coef_ref, f32[1,16,128]{2,1,0:T(8,128)S(1)} %bitcast.87, ...), custom_call_target="tpu_custom_call" | custom-call | flops 16777216 | bytes 31981568 | tf_op jit(solution)/shard_map/cond/branch_0_fun/sens_block/pallas_call | solution.py:323
  269.8 0.8 collective-permute-start.4
  270.6 0.8 collective-permute-done.4
  271.4 4.2 %collective-permute-start.5 = (f32[1,16,128]{2,1,0:T(8,128)S(1)}, f32[1,16,128]{2,1,0:T(8,128)S(1)}, u32[]{:S(2)}, u32[]{:S(2)}) collective-permute-start(f32[1,16,128]{2,1,0:T(8,128)S(1)} %add.85), channel_id=1, source_target_pairs={{0,2},{1,3},{2,0},{3,1},{4,6},{5,7},{6,4},{7,5},{8,10},{9,11},{10,... | collective-permute-start | bytes 24584 | tf_op jit(solution)/shard_map/cond/branch_0_fun/ppermute | solution.py:440
  275.7 1.6 collective-permute-done.5
  277.3 8.3 %collective-permute-start.8 = (f32[1,16,128]{2,1,0:T(8,128)S(1)}, f32[1,16,128]{2,1,0:T(8,128)S(1)}, u32[]{:S(2)}, u32[]{:S(2)}) collective-permute-start(f32[1,16,128]{2,1,0:T(8,128)S(1)} %add.86), channel_id=1, source_target_pairs={{0,12},{1,13},{2,14},{3,15},{4,8},{5,9},{6,10},{7,11},{8,4},{9,5},... | collective-permute-start | bytes 24584 | tf_op jit(solution)/shard_map/cond/branch_0_fun/ppermute | solution.py:440
  285.7 1.0 collective-permute-start.7
  286.7 0.6 collective-permute-start.6
  287.2 0.1 collective-permute-done.8
  287.3 2.9 collective-permute-done.7
  290.2 0.1 collective-permute-done.6
  290.3 8.7 %scaled.3 = (bf16[2048,4,512]{2,1,0:T(4,128)(2,1)}, f32[4,128]{1,0:T(4,128)}) custom-call(f32[16,128]{1,0:T(8,128)S(1)} %bitcast.84, f32[16,128]{1,0:T(8,128)S(1)} %add_bitcast_fusion.1.theirs_ref, f32[8192,128]{1,0:T(8,128)} %get-tuple-element.69.refs_0_, f32[8192,128]{1,0:T(8,128)} %get-tuple-element.70.refs_1_, f32[8192,128]{1,0:T(8,128)} %get-tuple-element.71.refs_2_, ...), custom_call_target="tpu_custom_call" | custom-call | tf_op jit(solution)/shard_map/cond/branch_0_fun/scaled/pallas_call | solution.py:411
  (15 shorter events, 0.2 us)
Async XLA Ops:
  0.6 10.2 %copy-start = (s32[2048,4]{0,1:T(4,128)S(1)}, s32[2048,4]{0,1:T(4,128)}, u32[]{:S(2)}) copy-start(s32[2048,4]{0,1:T(4,128)} %param.14) | copy-start | bytes 98308
  0.6 10.2 %copy-start.1 = (f32[512]{0:T(512)S(1)}, f32[512]{0:T(512)}, u32[]{:S(2)}) copy-start(f32[512]{0:T(512)} %param.13) | copy-start | bytes 6148
  0.7 10.2 %copy-start.2 = (f32[512]{0:T(512)S(1)}, f32[512]{0:T(512)}, u32[]{:S(2)}) copy-start(f32[512]{0:T(512)} %param.12) | copy-start | bytes 6148
  0.7 10.2 %copy-start.3 = (f32[512]{0:T(512)S(1)}, f32[512]{0:T(512)}, u32[]{:S(2)}) copy-start(f32[512]{0:T(512)} %param.10) | copy-start | bytes 6148
  0.7 10.2 %copy-start.4 = (f32[512]{0:T(512)S(1)}, f32[512]{0:T(512)}, u32[]{:S(2)}) copy-start(f32[512]{0:T(512)} %param.11) | copy-start | bytes 6148
  10.8 193.8 %all-to-all-start = ((bf16[16,3,224,384]{3,2,1,0:T(8,128)(2,1)}), bf16[16,3,224,384]{3,2,1,0:T(8,128)(2,1)}, u32[]{:S(2)}, u32[]{:S(2)}) async-start(bf16[16,3,224,384]{3,2,1,0:T(8,128)(2,1)} %get-tuple-element.52), calls=%async_computation | async-start | bytes 16515072 | tf_op jit(solution)/shard_map/cond/branch_0_fun/all_to_all | solution.py:520
  26.0 2.6 collective-permute-start
  29.9 47.2 %collective-permute-start.1 = (bf16[4,3,40,512]{3,2,1,0:T(8,128)(2,1)S(1)}, bf16[4,3,40,512]{3,2,1,0:T(8,128)(2,1)S(1)}, u32[]{:S(2)}, u32[]{:S(2)}) collective-permute-start(bf16[4,3,40,512]{3,2,1,0:T(8,128)(2,1)S(1)} %dynamic-slice_bitcast_fusion.1), channel_id=1, source_target_pairs={{0,2},{1,3},{2,0},{3,1},{4,6},{5,7},{6,4},{7,5},{8,10},{9,11},{10,... | collective-permute-start | bytes 1474568 | tf_op jit(solution)/shard_map/cond/branch_0_fun/ppermute | solution.py:475
  77.2 80.2 %collective-permute-start.2 = (bf16[2,3,40,512]{3,2,1,0:T(8,128)(2,1)S(1)}, bf16[2,3,40,512]{3,2,1,0:T(8,128)(2,1)S(1)}, u32[]{:S(2)}, u32[]{:S(2)}) collective-permute-start(bf16[2,3,40,512]{3,2,1,0:T(8,128)(2,1)S(1)} %dynamic-slice_bitcast_fusion.2), channel_id=1, source_target_pairs={{0,4},{1,5},{2,6},{3,7},{4,0},{5,1},{6,2},{7,3},{8,12},{9,13},{10,... | collective-permute-start | bytes 737288 | tf_op jit(solution)/shard_map/cond/branch_0_fun/ppermute | solution.py:475
  157.5 47.1 %collective-permute-start.3 = (bf16[1,3,40,512]{3,2,1,0:T(8,128)(2,1)S(1)}, bf16[1,3,40,512]{3,2,1,0:T(8,128)(2,1)S(1)}, u32[]{:S(2)}, u32[]{:S(2)}) collective-permute-start(bf16[1,3,40,512]{3,2,1,0:T(8,128)(2,1)S(1)} %constant_dynamic-slice_fusion), channel_id=1, source_target_pairs={{0,8},{1,9},{2,10},{3,11},{4,12},{5,13},{6,14},{7,15},{8,0},{9,1},... | collective-permute-start | bytes 368648 | tf_op jit(solution)/shard_map/cond/branch_0_fun/ppermute | solution.py:475
  204.7 56.2 %all-to-all-start.1 = ((bf16[16,3,224,128]{3,2,1,0:T(8,128)(2,1)}), bf16[16,3,224,128]{3,2,1,0:T(8,128)(2,1)S(1)}, u32[]{:S(2)}, u32[]{:S(2)}) async-start(bf16[16,3,224,128]{3,2,1,0:T(8,128)(2,1)} %send_order.5), calls=%async_computation.1 | async-start | bytes 5505024 | tf_op jit(solution)/shard_map/cond/branch_0_fun/all_to_all | solution.py:520
  269.8 1.7 collective-permute-start.4
  271.4 5.9 %collective-permute-start.5 = (f32[1,16,128]{2,1,0:T(8,128)S(1)}, f32[1,16,128]{2,1,0:T(8,128)S(1)}, u32[]{:S(2)}, u32[]{:S(2)}) collective-permute-start(f32[1,16,128]{2,1,0:T(8,128)S(1)} %add.85), channel_id=1, source_target_pairs={{0,2},{1,3},{2,0},{3,1},{4,6},{5,7},{6,4},{7,5},{8,10},{9,11},{10,... | collective-permute-start | bytes 24584 | tf_op jit(solution)/shard_map/cond/branch_0_fun/ppermute | solution.py:440
  277.3 10.0 %collective-permute-start.8 = (f32[1,16,128]{2,1,0:T(8,128)S(1)}, f32[1,16,128]{2,1,0:T(8,128)S(1)}, u32[]{:S(2)}, u32[]{:S(2)}) collective-permute-start(f32[1,16,128]{2,1,0:T(8,128)S(1)} %add.86), channel_id=1, source_target_pairs={{0,12},{1,13},{2,14},{3,15},{4,8},{5,9},{6,10},{7,11},{8,4},{9,5},... | collective-permute-start | bytes 24584 | tf_op jit(solution)/shard_map/cond/branch_0_fun/ppermute | solution.py:440
  285.7 4.5 %collective-permute-start.7 = (f32[1,16,128]{2,1,0:T(8,128)S(1)}, f32[1,16,128]{2,1,0:T(8,128)S(1)}, u32[]{:S(2)}, u32[]{:S(2)}) collective-permute-start(f32[1,16,128]{2,1,0:T(8,128)S(1)} %add.86), channel_id=1, source_target_pairs={{0,8},{1,9},{2,10},{3,11},{4,12},{5,13},{6,14},{7,15},{8,0},{9,1},... | collective-permute-start | bytes 24584 | tf_op jit(solution)/shard_map/cond/branch_0_fun/ppermute | solution.py:440
  286.7 3.7 %collective-permute-start.6 = (f32[1,16,128]{2,1,0:T(8,128)S(1)}, f32[1,16,128]{2,1,0:T(8,128)S(1)}, u32[]{:S(2)}, u32[]{:S(2)}) collective-permute-start(f32[1,16,128]{2,1,0:T(8,128)S(1)} %add.86), channel_id=1, source_target_pairs={{0,4},{1,5},{2,6},{3,7},{4,0},{5,1},{6,2},{7,3},{8,12},{9,13},{10,... | collective-permute-start | bytes 24584 | tf_op jit(solution)/shard_map/cond/branch_0_fun/ppermute | solution.py:440

commit v2 on v1

--- a/solution.py
+++ b/solution.py
@@ -13,9 +13,9 @@
 FILL_STEPS = 4
 GROUP_ROWS = 512
 SCALE_ROWS = 256
-ROW_TILE = 8
+ROW_TILE = 16
 KEEPS = (28, 30)
-POOL = 5
+POOL = 6
 PAD = 4
 MIB = 1 << 20
 VMEM_LIMIT = 60 * MIB

time: 300 us -> 301 us (level)
  no operation moved by 1% of the time
where the time goes in v2:
time: 301 us; the launch traced here: 300 us
  waiting for transfers between devices  184 us (61%)
  Pallas kernels  77.6 us (26%)
  starting transfers between devices  33.1 us (11%)
    ppermute x4, waiting for transfers between devices, scatter_over_cells(): x = kept + lax.ppermute(sent, 'cell', [(i, i ^ bit) for i in range(shards)])  162 us
    pallas_call x4, Pallas kernels, sens_block(): pl.pallas_call(functools.partial(sens_kernel, shards // fill_steps, fill_...  45.1 us
    all_to_all x2, waiting for transfers between devices, transfer_and_solve(): lax.all_to_all(ready, 'cell', split_axis=0, concat_axis=0, tiled=True)  16.1 us
    ppermute x5, starting transfers between devices, sum_over_cells(): lax.ppermute(x, 'cell', [(i, i ^ k * unit) for i in range(shards)])  15 us
    pallas_call x2, Pallas kernels, send_order(): pl.pallas_call(functools.partial(send_order_kernel if rank is None else s...  12.2 us
    all_to_all x2, starting transfers between devices, transfer_and_solve(): lax.all_to_all(ready, 'cell', split_axis=0, concat_axis=0, tiled=True)  11.2 us
    pallas_call x1, Pallas kernels, send_first(): pl.pallas_call(functools.partial(send_first_kernel, keeps, pool), in_spec...  9.45 us
    pallas_call x1, Pallas kernels, scaled(): pl.pallas_call(functools.partial(scale_kernel, inverse, len(far)), in_spe...  8.71 us
  transfers between devices with their start and end apart: 11, of which 10 were waited for; matrix products, arithmetic and copies ran while one was open for 1% of the time, Pallas kernels for 17%

profile of v2, /device:TPU:0, one launch (start us, length us, event | category | flops | bytes accessed | tf_op | source)
XLA Modules:
  0.0 300.5 jit_solution(12902875975865893591)
XLA Ops:
  0.6 0.0 copy-start
  0.6 0.0 copy-start.1
  0.7 0.0 copy-start.2
  0.7 0.0 copy-start.3
  0.7 0.0 copy-start.4
  0.7 9.4 %send_first.1 = (bf16[16,3,224,384]{3,2,1,0:T(8,128)(2,1)}, bf16[16,3,240,384]{3,2,1,0:T(8,128)(2,1)}, f32[32,128]{1,0:T(8,128)S(1)}, f32[32,128]{1,0:T(8,128)S(1)}, f32[32,128]{1,0:T(8,128)S(1)}, /*index=5*/s32[1]{0:T(128)}) custom-call(bf16[3,256,8192]{2,1,0:T(8,128)(2,1)} %bitcast.90, s32[4,2048]{1,0:T(4,128)} %bitcast.100), custom_call_target="tpu_custom_call" | custom-call | tf_op jit(solution)/shard_map/send_first/pallas_call | solution.py:187
  10.8 0.0 copy-done
  10.8 0.0 copy-done.1
  10.8 0.0 copy-done.2
  10.8 0.0 copy-done.3
  10.8 0.0 copy-done.4
  10.8 289.5 %conditional.1 = (bf16[2048,4,512]{2,1,0:T(4,128)(2,1)}, f32[512]{0:T(512)}) conditional(s32[]{:T(128)} %bitcast.54, (bf16[3,256,8192]{2,1,0:T(8,128)(2,1)}, f32[32,128]{1,0:T(8,128)S(1)}, bf16[16,3,224,384]{3,2,1,0:T(8,128)(2,1)}, f32[32,128]{1,0:T(8,128)S(1)}, s32[4,2048]{1,0:T(4,128)S(1)}, /*index=5*/f32[32,128]{1,0:T(8,128)S(1)}, ...), branch_computations={%region_0.1_spmd, %region_1.2_spmd, %region_2.3_spmd} | conditional | flops 68227688 | bytes 212825584 | solution.py:552
  10.8 7.4 %all-to-all-start = ((bf16[16,3,224,384]{3,2,1,0:T(8,128)(2,1)}), bf16[16,3,224,384]{3,2,1,0:T(8,128)(2,1)}, u32[]{:S(2)}, u32[]{:S(2)}) async-start(bf16[16,3,224,384]{3,2,1,0:T(8,128)(2,1)} %get-tuple-element.52), calls=%async_computation | async-start | bytes 16515072 | tf_op jit(solution)/shard_map/cond/branch_0_fun/all_to_all | solution.py:520
  18.3 6.5 %send_order.6 = bf16[16,3,48,512]{3,2,1,0:T(8,128)(2,1)} custom-call(bf16[3,256,8192]{2,1,0:T(8,128)(2,1)} %get-tuple-element.50.fields_ref, f32[32,128]{1,0:T(8,128)S(1)} %get-tuple-element.53.rank_ref), custom_call_target="tpu_custom_call" | custom-call | bytes 25165824 | tf_op jit(solution)/shard_map/cond/branch_0_fun/send_order/pallas_call | solution.py:217
  24.8 1.4 dynamic-slice_bitcast_fusion
  26.2 0.4 collective-permute-start
  26.6 2.5 collective-permute-done
  29.1 1.4 bitcast_add_fusion
  30.5 0.1 dynamic-slice_bitcast_fusion.1
  30.5 1.9 collective-permute-start.1
  32.5 58.8 %collective-permute-done.1 = bf16[4,3,48,512]{3,2,1,0:T(8,128)(2,1)S(1)} collective-permute-done((bf16[4,3,48,512]{3,2,1,0:T(8,128)(2,1)S(1)}, bf16[4,3,48,512]{3,2,1,0:T(8,128)(2,1)S(1)}, u32[]{:S(2)}, u32[]{:S(2)}) %collective-permute-start.1) | collective-permute-done | bytes 589856 | tf_op jit(solution)/shard_map/cond/branch_0_fun/ppermute | solution.py:475
  91.3 0.1 bitcast_add_fusion.1
  91.4 0.1 collective-permute-start.2
  91.5 2.1 table_rows.2
  93.7 0.8 copy.11
  94.4 5.7 %send_order.5 = bf16[16,3,224,128]{3,2,1,0:T(8,128)(2,1)} custom-call(bf16[3,256,8192]{2,1,0:T(8,128)(2,1)} %get-tuple-element.50.fields_ref, f32[32,128]{1,0:T(8,128)S(1)} %get-tuple-element.51.rank_ref), custom_call_target="tpu_custom_call" | custom-call | bytes 6291456 | tf_op jit(solution)/shard_map/cond/branch_0_fun/send_order/pallas_call | solution.py:217
  100.2 58.4 %collective-permute-done.2 = bf16[2,3,48,512]{3,2,1,0:T(8,128)(2,1)S(1)} collective-permute-done((bf16[2,3,48,512]{3,2,1,0:T(8,128)(2,1)S(1)}, bf16[2,3,48,512]{3,2,1,0:T(8,128)(2,1)S(1)}, u32[]{:S(2)}, u32[]{:S(2)}) %collective-permute-start.2) | collective-permute-done | bytes 294944 | tf_op jit(solution)/shard_map/cond/branch_0_fun/ppermute | solution.py:475
  158.6 4.6 %collective-permute-start.3 = (bf16[1,3,48,512]{3,2,1,0:T(8,128)(2,1)S(1)}, bf16[1,3,48,512]{3,2,1,0:T(8,128)(2,1)S(1)}, u32[]{:S(2)}, u32[]{:S(2)}) collective-permute-start(bf16[1,3,48,512]{3,2,1,0:T(8,128)(2,1)S(1)} %constant_dynamic-slice_fusion), channel_id=1, source_target_pairs={{0,8},{1,9},{2,10},{3,11},{4,12},{5,13},{6,14},{7,15},{8,0},{9,1},... | collective-permute-start | bytes 442376 | tf_op jit(solution)/shard_map/cond/branch_0_fun/ppermute | solution.py:475
  163.2 0.1 stack.79
  163.3 42.4 %collective-permute-done.3 = bf16[1,3,48,512]{3,2,1,0:T(8,128)(2,1)S(1)} collective-permute-done((bf16[1,3,48,512]{3,2,1,0:T(8,128)(2,1)S(1)}, bf16[1,3,48,512]{3,2,1,0:T(8,128)(2,1)S(1)}, u32[]{:S(2)}, u32[]{:S(2)}) %collective-permute-start.3) | collective-permute-done | bytes 147488 | tf_op jit(solution)/shard_map/cond/branch_0_fun/ppermute | solution.py:475
  205.7 0.0 all-to-all-done.fields_ref
  205.7 3.7 %all-to-all-start.1 = ((bf16[16,3,224,128]{3,2,1,0:T(8,128)(2,1)}), bf16[16,3,224,128]{3,2,1,0:T(8,128)(2,1)S(1)}, u32[]{:S(2)}, u32[]{:S(2)}) async-start(bf16[16,3,224,128]{3,2,1,0:T(8,128)(2,1)} %send_order.5), calls=%async_computation.1 | async-start | bytes 5505024 | tf_op jit(solution)/shard_map/cond/branch_0_fun/all_to_all | solution.py:520
  209.5 12.1 %sens_block.12 = (f32[8192,128]{1,0:T(8,128)}, f32[4,4,128]{2,1,0:T(4,128)S(1)}) custom-call(s32[8192]{0:T(1024)S(1)} %bitcast.72, bf16[16,3,224,384]{3,2,1,0:T(8,128)(2,1)} %all-to-all-done.fields_ref, f32[16,128]{1,0:T(8,128)S(1)} %get-tuple-element.133.coef_ref, f32[4,4,128]{2,1,0:T(4,128)S(1)} %broadcast_3_before_ref.0.before_ref, ...), custom_call_target="tpu_custom_call" | custom-call | flops 16777216 | bytes 31981568 | tf_op jit(solution)/shard_map/cond/branch_0_fun/sens_block/pallas_call | solution.py:323
  221.7 12.1 %sens_block.13 = (f32[8192,128]{1,0:T(8,128)}, f32[4,4,128]{2,1,0:T(4,128)S(1)}) custom-call(s32[8192]{0:T(1024)S(1)} %bitcast.73, bf16[16,3,224,384]{3,2,1,0:T(8,128)(2,1)} %all-to-all-done.fields_ref, f32[16,128]{1,0:T(8,128)S(1)} %get-tuple-element.134.coef_ref, f32[4,4,128]{2,1,0:T(4,128)S(1)} %get-tuple-element.65.before_ref, ...), custom_call_target="tpu_custom_call" | custom-call | flops 16777216 | bytes 31981568 | tf_op jit(solution)/shard_map/cond/branch_0_fun/sens_block/pallas_call | solution.py:323
  233.7 12.1 %sens_block.14 = (f32[8192,128]{1,0:T(8,128)}, f32[4,4,128]{2,1,0:T(4,128)S(1)}) custom-call(s32[8192]{0:T(1024)S(1)} %bitcast.74, bf16[16,3,224,384]{3,2,1,0:T(8,128)(2,1)} %all-to-all-done.fields_ref, f32[16,128]{1,0:T(8,128)S(1)} %get-tuple-element.135.coef_ref, f32[4,4,128]{2,1,0:T(4,128)S(1)} %get-tuple-element.66.before_ref, ...), custom_call_target="tpu_custom_call" | custom-call | flops 16777216 | bytes 31981568 | tf_op jit(solution)/shard_map/cond/branch_0_fun/sens_block/pallas_call | solution.py:323
  245.8 16.1 %all-to-all-done.1.fields_ref = bf16[16,3,224,128]{3,2,1,0:T(8,128)(2,1)S(1)} async-done(((bf16[16,3,224,128]{3,2,1,0:T(8,128)(2,1)}), bf16[16,3,224,128]{3,2,1,0:T(8,128)(2,1)S(1)}, u32[]{:S(2)}, u32[]{:S(2)}) %all-to-all-start.1) | async-done | bytes 2752544 | tf_op jit(solution)/shard_map/cond/branch_0_fun/all_to_all | solution.py:520
  261.9 8.9 %sens_block.15 = (f32[8192,128]{1,0:T(8,128)S(1)}, f32[1,16,128]{2,1,0:T(8,128)S(1)}) custom-call(s32[8192]{0:T(1024)S(1)} %bitcast.75, bf16[16,3,224,128]{3,2,1,0:T(8,128)(2,1)S(1)} %all-to-all-done.1.fields_ref, f32[16,128]{1,0:T(8,128)S(1)} %get-tuple-element.136.coef_ref, f32[1,16,128]{2,1,0:T(8,128)S(1)} %bitcast.87, ...), custom_call_target="tpu_custom_call" | custom-call | flops 16777216 | bytes 31981568 | tf_op jit(solution)/shard_map/cond/branch_0_fun/sens_block/pallas_call | solution.py:323
  270.8 0.8 collective-permute-start.4
  271.7 0.8 collective-permute-done.4
  272.5 4.2 %collective-permute-start.5 = (f32[1,16,128]{2,1,0:T(8,128)S(1)}, f32[1,16,128]{2,1,0:T(8,128)S(1)}, u32[]{:S(2)}, u32[]{:S(2)}) collective-permute-start(f32[1,16,128]{2,1,0:T(8,128)S(1)} %add.85), channel_id=1, source_target_pairs={{0,2},{1,3},{2,0},{3,1},{4,6},{5,7},{6,4},{7,5},{8,10},{9,11},{10,... | collective-permute-start | bytes 24584 | tf_op jit(solution)/shard_map/cond/branch_0_fun/ppermute | solution.py:440
  276.7 1.6 collective-permute-done.5
  278.4 8.3 %collective-permute-start.8 = (f32[1,16,128]{2,1,0:T(8,128)S(1)}, f32[1,16,128]{2,1,0:T(8,128)S(1)}, u32[]{:S(2)}, u32[]{:S(2)}) collective-permute-start(f32[1,16,128]{2,1,0:T(8,128)S(1)} %add.86), channel_id=1, source_target_pairs={{0,12},{1,13},{2,14},{3,15},{4,8},{5,9},{6,10},{7,11},{8,4},{9,5},... | collective-permute-start | bytes 24584 | tf_op jit(solution)/shard_map/cond/branch_0_fun/ppermute | solution.py:440
  286.7 1.0 collective-permute-start.7
  287.7 0.6 collective-permute-start.6
  288.3 0.1 collective-permute-done.8
  288.3 2.9 collective-permute-done.7
  291.3 0.1 collective-permute-done.6
  291.4 8.7 %scaled.3 = (bf16[2048,4,512]{2,1,0:T(4,128)(2,1)}, f32[4,128]{1,0:T(4,128)}) custom-call(f32[16,128]{1,0:T(8,128)S(1)} %bitcast.84, f32[16,128]{1,0:T(8,128)S(1)} %add_bitcast_fusion.1.theirs_ref, f32[8192,128]{1,0:T(8,128)} %get-tuple-element.69.refs_0_, f32[8192,128]{1,0:T(8,128)} %get-tuple-element.70.refs_1_, f32[8192,128]{1,0:T(8,128)} %get-tuple-element.71.refs_2_, ...), custom_call_target="tpu_custom_call" | custom-call | tf_op jit(solution)/shard_map/cond/branch_0_fun/scaled/pallas_call | solution.py:411
  (14 shorter events, 0.2 us)
Async XLA Ops:
  0.6 10.2 %copy-start = (s32[2048,4]{0,1:T(4,128)S(1)}, s32[2048,4]{0,1:T(4,128)}, u32[]{:S(2)}) copy-start(s32[2048,4]{0,1:T(4,128)} %param.14) | copy-start | bytes 98308
  0.6 10.2 %copy-start.1 = (f32[512]{0:T(512)S(1)}, f32[512]{0:T(512)}, u32[]{:S(2)}) copy-start(f32[512]{0:T(512)} %param.13) | copy-start | bytes 6148
  0.7 10.2 %copy-start.2 = (f32[512]{0:T(512)S(1)}, f32[512]{0:T(512)}, u32[]{:S(2)}) copy-start(f32[512]{0:T(512)} %param.12) | copy-start | bytes 6148
  0.7 10.2 %copy-start.3 = (f32[512]{0:T(512)S(1)}, f32[512]{0:T(512)}, u32[]{:S(2)}) copy-start(f32[512]{0:T(512)} %param.10) | copy-start | bytes 6148
  0.7 10.2 %copy-start.4 = (f32[512]{0:T(512)S(1)}, f32[512]{0:T(512)}, u32[]{:S(2)}) copy-start(f32[512]{0:T(512)} %param.11) | copy-start | bytes 6148
  10.8 194.9 %all-to-all-start = ((bf16[16,3,224,384]{3,2,1,0:T(8,128)(2,1)}), bf16[16,3,224,384]{3,2,1,0:T(8,128)(2,1)}, u32[]{:S(2)}, u32[]{:S(2)}) async-start(bf16[16,3,224,384]{3,2,1,0:T(8,128)(2,1)} %get-tuple-element.52), calls=%async_computation | async-start | bytes 16515072 | tf_op jit(solution)/shard_map/cond/branch_0_fun/all_to_all | solution.py:520
  26.2 2.9 collective-permute-start
  30.5 60.7 %collective-permute-start.1 = (bf16[4,3,48,512]{3,2,1,0:T(8,128)(2,1)S(1)}, bf16[4,3,48,512]{3,2,1,0:T(8,128)(2,1)S(1)}, u32[]{:S(2)}, u32[]{:S(2)}) collective-permute-start(bf16[4,3,48,512]{3,2,1,0:T(8,128)(2,1)S(1)} %dynamic-slice_bitcast_fusion.1), channel_id=1, source_target_pairs={{0,2},{1,3},{2,0},{3,1},{4,6},{5,7},{6,4},{7,5},{8,10},{9,11},{10,... | collective-permute-start | bytes 1769480 | tf_op jit(solution)/shard_map/cond/branch_0_fun/ppermute | solution.py:475
  91.4 67.2 %collective-permute-start.2 = (bf16[2,3,48,512]{3,2,1,0:T(8,128)(2,1)S(1)}, bf16[2,3,48,512]{3,2,1,0:T(8,128)(2,1)S(1)}, u32[]{:S(2)}, u32[]{:S(2)}) collective-permute-start(bf16[2,3,48,512]{3,2,1,0:T(8,128)(2,1)S(1)} %dynamic-slice_bitcast_fusion.2), channel_id=1, source_target_pairs={{0,4},{1,5},{2,6},{3,7},{4,0},{5,1},{6,2},{7,3},{8,12},{9,13},{10,... | collective-permute-start | bytes 884744 | tf_op jit(solution)/shard_map/cond/branch_0_fun/ppermute | solution.py:475
  158.6 47.1 %collective-permute-start.3 = (bf16[1,3,48,512]{3,2,1,0:T(8,128)(2,1)S(1)}, bf16[1,3,48,512]{3,2,1,0:T(8,128)(2,1)S(1)}, u32[]{:S(2)}, u32[]{:S(2)}) collective-permute-start(bf16[1,3,48,512]{3,2,1,0:T(8,128)(2,1)S(1)} %constant_dynamic-slice_fusion), channel_id=1, source_target_pairs={{0,8},{1,9},{2,10},{3,11},{4,12},{5,13},{6,14},{7,15},{8,0},{9,1},... | collective-permute-start | bytes 442376 | tf_op jit(solution)/shard_map/cond/branch_0_fun/ppermute | solution.py:475
  205.7 56.2 %all-to-all-start.1 = ((bf16[16,3,224,128]{3,2,1,0:T(8,128)(2,1)}), bf16[16,3,224,128]{3,2,1,0:T(8,128)(2,1)S(1)}, u32[]{:S(2)}, u32[]{:S(2)}) async-start(bf16[16,3,224,128]{3,2,1,0:T(8,128)(2,1)} %send_order.5), calls=%async_computation.1 | async-start | bytes 5505024 | tf_op jit(solution)/shard_map/cond/branch_0_fun/all_to_all | solution.py:520
  270.8 1.7 collective-permute-start.4
  272.5 5.9 %collective-permute-start.5 = (f32[1,16,128]{2,1,0:T(8,128)S(1)}, f32[1,16,128]{2,1,0:T(8,128)S(1)}, u32[]{:S(2)}, u32[]{:S(2)}) collective-permute-start(f32[1,16,128]{2,1,0:T(8,128)S(1)} %add.85), channel_id=1, source_target_pairs={{0,2},{1,3},{2,0},{3,1},{4,6},{5,7},{6,4},{7,5},{8,10},{9,11},{10,... | collective-permute-start | bytes 24584 | tf_op jit(solution)/shard_map/cond/branch_0_fun/ppermute | solution.py:440
  278.4 10.0 %collective-permute-start.8 = (f32[1,16,128]{2,1,0:T(8,128)S(1)}, f32[1,16,128]{2,1,0:T(8,128)S(1)}, u32[]{:S(2)}, u32[]{:S(2)}) collective-permute-start(f32[1,16,128]{2,1,0:T(8,128)S(1)} %add.86), channel_id=1, source_target_pairs={{0,12},{1,13},{2,14},{3,15},{4,8},{5,9},{6,10},{7,11},{8,4},{9,5},... | collective-permute-start | bytes 24584 | tf_op jit(solution)/shard_map/cond/branch_0_fun/ppermute | solution.py:440
  286.7 4.5 %collective-permute-start.7 = (f32[1,16,128]{2,1,0:T(8,128)S(1)}, f32[1,16,128]{2,1,0:T(8,128)S(1)}, u32[]{:S(2)}, u32[]{:S(2)}) collective-permute-start(f32[1,16,128]{2,1,0:T(8,128)S(1)} %add.86), channel_id=1, source_target_pairs={{0,8},{1,9},{2,10},{3,11},{4,12},{5,13},{6,14},{7,15},{8,0},{9,1},... | collective-permute-start | bytes 24584 | tf_op jit(solution)/shard_map/cond/branch_0_fun/ppermute | solution.py:440
  287.7 3.7 %collective-permute-start.6 = (f32[1,16,128]{2,1,0:T(8,128)S(1)}, f32[1,16,128]{2,1,0:T(8,128)S(1)}, u32[]{:S(2)}, u32[]{:S(2)}) collective-permute-start(f32[1,16,128]{2,1,0:T(8,128)S(1)} %add.86), channel_id=1, source_target_pairs={{0,4},{1,5},{2,6},{3,7},{4,0},{5,1},{6,2},{7,3},{8,12},{9,13},{10,... | collective-permute-start | bytes 24584 | tf_op jit(solution)/shard_map/cond/branch_0_fun/ppermute | solution.py:440

commit v3 on v2

--- a/solution.py
+++ b/solution.py
@@ -12,7 +12,7 @@
 UNROLL = 16
 FILL_STEPS = 4
 GROUP_ROWS = 512
-SCALE_ROWS = 256
+SCALE_ROWS = 512
 ROW_TILE = 16
 KEEPS = (28, 30)
 POOL = 6

time: 301 us -> 301 us (level)
  no operation moved by 1% of the time
where the time goes in v3:
time: 301 us; the launch traced here: 300 us
  waiting for transfers between devices  184 us (61%)
  Pallas kernels  77.3 us (26%)
  starting transfers between devices  33.1 us (11%)
    ppermute x4, waiting for transfers between devices, scatter_over_cells(): x = kept + lax.ppermute(sent, 'cell', [(i, i ^ bit) for i in range(shards)])  162 us
    pallas_call x4, Pallas kernels, sens_block(): pl.pallas_call(functools.partial(sens_kernel, shards // fill_steps, fill_...  45.1 us
    all_to_all x2, waiting for transfers between devices, transfer_and_solve(): lax.all_to_all(ready, 'cell', split_axis=0, concat_axis=0, tiled=True)  16.1 us
    ppermute x5, starting transfers between devices, sum_over_cells(): lax.ppermute(x, 'cell', [(i, i ^ k * unit) for i in range(shards)])  15 us
    pallas_call x2, Pallas kernels, send_order(): pl.pallas_call(functools.partial(send_order_kernel if rank is None else s...  12.2 us
    all_to_all x2, starting transfers between devices, transfer_and_solve(): lax.all_to_all(ready, 'cell', split_axis=0, concat_axis=0, tiled=True)  11.2 us
    pallas_call x1, Pallas kernels, send_first(): pl.pallas_call(functools.partial(send_first_kernel, keeps, pool), in_spec...  9.45 us
    pallas_call x1, Pallas kernels, scaled(): pl.pallas_call(functools.partial(scale_kernel, inverse, len(far)), in_spe...  8.45 us
  transfers between devices with their start and end apart: 11, of which 10 were waited for; matrix products, arithmetic and copies ran while one was open for 1% of the time, Pallas kernels for 17%

profile of v3, /device:TPU:0, one launch (start us, length us, event | category | flops | bytes accessed | tf_op | source)
XLA Modules:
  0.0 300.2 jit_solution(9164306501281246713)
XLA Ops:
  0.6 0.0 copy-start
  0.6 0.0 copy-start.1
  0.7 0.0 copy-start.2
  0.7 0.0 copy-start.3
  0.7 0.0 copy-start.4
  0.7 9.4 %send_first.1 = (bf16[16,3,224,384]{3,2,1,0:T(8,128)(2,1)}, bf16[16,3,240,384]{3,2,1,0:T(8,128)(2,1)}, f32[32,128]{1,0:T(8,128)S(1)}, f32[32,128]{1,0:T(8,128)S(1)}, f32[32,128]{1,0:T(8,128)S(1)}, /*index=5*/s32[1]{0:T(128)}) custom-call(bf16[3,256,8192]{2,1,0:T(8,128)(2,1)} %bitcast.90, s32[4,2048]{1,0:T(4,128)} %bitcast.100), custom_call_target="tpu_custom_call" | custom-call | tf_op jit(solution)/shard_map/send_first/pallas_call | solution.py:187
  10.8 0.0 copy-done
  10.8 0.0 copy-done.1
  10.8 0.0 copy-done.2
  10.8 0.0 copy-done.3
  10.8 0.0 copy-done.4
  10.8 289.2 %conditional.1 = (bf16[2048,4,512]{2,1,0:T(4,128)(2,1)}, f32[512]{0:T(512)}) conditional(s32[]{:T(128)} %bitcast.54, (bf16[3,256,8192]{2,1,0:T(8,128)(2,1)}, f32[32,128]{1,0:T(8,128)S(1)}, bf16[16,3,224,384]{3,2,1,0:T(8,128)(2,1)}, f32[32,128]{1,0:T(8,128)S(1)}, s32[4,2048]{1,0:T(4,128)S(1)}, /*index=5*/f32[32,128]{1,0:T(8,128)S(1)}, ...), branch_computations={%region_0.1_spmd, %region_1.2_spmd, %region_2.3_spmd} | conditional | flops 68227688 | bytes 212825584 | solution.py:552
  10.8 7.4 %all-to-all-start = ((bf16[16,3,224,384]{3,2,1,0:T(8,128)(2,1)}), bf16[16,3,224,384]{3,2,1,0:T(8,128)(2,1)}, u32[]{:S(2)}, u32[]{:S(2)}) async-start(bf16[16,3,224,384]{3,2,1,0:T(8,128)(2,1)} %get-tuple-element.52), calls=%async_computation | async-start | bytes 16515072 | tf_op jit(solution)/shard_map/cond/branch_0_fun/all_to_all | solution.py:520
  18.3 6.5 %send_order.6 = bf16[16,3,48,512]{3,2,1,0:T(8,128)(2,1)} custom-call(bf16[3,256,8192]{2,1,0:T(8,128)(2,1)} %get-tuple-element.50.fields_ref, f32[32,128]{1,0:T(8,128)S(1)} %get-tuple-element.53.rank_ref), custom_call_target="tpu_custom_call" | custom-call | bytes 25165824 | tf_op jit(solution)/shard_map/cond/branch_0_fun/send_order/pallas_call | solution.py:217
  24.8 1.4 dynamic-slice_bitcast_fusion
  26.2 0.4 collective-permute-start
  26.6 2.5 collective-permute-done
  29.1 1.4 bitcast_add_fusion
  30.5 0.1 dynamic-slice_bitcast_fusion.1
  30.5 1.9 collective-permute-start.1
  32.5 58.8 %collective-permute-done.1 = bf16[4,3,48,512]{3,2,1,0:T(8,128)(2,1)S(1)} collective-permute-done((bf16[4,3,48,512]{3,2,1,0:T(8,128)(2,1)S(1)}, bf16[4,3,48,512]{3,2,1,0:T(8,128)(2,1)S(1)}, u32[]{:S(2)}, u32[]{:S(2)}) %collective-permute-start.1) | collective-permute-done | bytes 589856 | tf_op jit(solution)/shard_map/cond/branch_0_fun/ppermute | solution.py:475
  91.3 0.1 bitcast_add_fusion.1
  91.4 0.1 collective-permute-start.2
  91.5 2.1 table_rows.2
  93.7 0.8 copy.11
  94.4 5.7 %send_order.5 = bf16[16,3,224,128]{3,2,1,0:T(8,128)(2,1)} custom-call(bf16[3,256,8192]{2,1,0:T(8,128)(2,1)} %get-tuple-element.50.fields_ref, f32[32,128]{1,0:T(8,128)S(1)} %get-tuple-element.51.rank_ref), custom_call_target="tpu_custom_call" | custom-call | bytes 6291456 | tf_op jit(solution)/shard_map/cond/branch_0_fun/send_order/pallas_call | solution.py:217
  100.2 58.4 %collective-permute-done.2 = bf16[2,3,48,512]{3,2,1,0:T(8,128)(2,1)S(1)} collective-permute-done((bf16[2,3,48,512]{3,2,1,0:T(8,128)(2,1)S(1)}, bf16[2,3,48,512]{3,2,1,0:T(8,128)(2,1)S(1)}, u32[]{:S(2)}, u32[]{:S(2)}) %collective-permute-start.2) | collective-permute-done | bytes 294944 | tf_op jit(solution)/shard_map/cond/branch_0_fun/ppermute | solution.py:475
  158.6 4.6 %collective-permute-start.3 = (bf16[1,3,48,512]{3,2,1,0:T(8,128)(2,1)S(1)}, bf16[1,3,48,512]{3,2,1,0:T(8,128)(2,1)S(1)}, u32[]{:S(2)}, u32[]{:S(2)}) collective-permute-start(bf16[1,3,48,512]{3,2,1,0:T(8,128)(2,1)S(1)} %constant_dynamic-slice_fusion), channel_id=1, source_target_pairs={{0,8},{1,9},{2,10},{3,11},{4,12},{5,13},{6,14},{7,15},{8,0},{9,1},... | collective-permute-start | bytes 442376 | tf_op jit(solution)/shard_map/cond/branch_0_fun/ppermute | solution.py:475
  163.2 0.1 stack.79
  163.3 42.4 %collective-permute-done.3 = bf16[1,3,48,512]{3,2,1,0:T(8,128)(2,1)S(1)} collective-permute-done((bf16[1,3,48,512]{3,2,1,0:T(8,128)(2,1)S(1)}, bf16[1,3,48,512]{3,2,1,0:T(8,128)(2,1)S(1)}, u32[]{:S(2)}, u32[]{:S(2)}) %collective-permute-start.3) | collective-permute-done | bytes 147488 | tf_op jit(solution)/shard_map/cond/branch_0_fun/ppermute | solution.py:475
  205.7 0.0 all-to-all-done.fields_ref
  205.7 3.7 %all-to-all-start.1 = ((bf16[16,3,224,128]{3,2,1,0:T(8,128)(2,1)}), bf16[16,3,224,128]{3,2,1,0:T(8,128)(2,1)S(1)}, u32[]{:S(2)}, u32[]{:S(2)}) async-start(bf16[16,3,224,128]{3,2,1,0:T(8,128)(2,1)} %send_order.5), calls=%async_computation.1 | async-start | bytes 5505024 | tf_op jit(solution)/shard_map/cond/branch_0_fun/all_to_all | solution.py:520
  209.5 12.1 %sens_block.12 = (f32[8192,128]{1,0:T(8,128)}, f32[4,4,128]{2,1,0:T(4,128)S(1)}) custom-call(s32[8192]{0:T(1024)S(1)} %bitcast.72, bf16[16,3,224,384]{3,2,1,0:T(8,128)(2,1)} %all-to-all-done.fields_ref, f32[16,128]{1,0:T(8,128)S(1)} %get-tuple-element.133.coef_ref, f32[4,4,128]{2,1,0:T(4,128)S(1)} %broadcast_3_before_ref.0.before_ref, ...), custom_call_target="tpu_custom_call" | custom-call | flops 16777216 | bytes 31981568 | tf_op jit(solution)/shard_map/cond/branch_0_fun/sens_block/pallas_call | solution.py:323
  221.7 12.1 %sens_block.13 = (f32[8192,128]{1,0:T(8,128)}, f32[4,4,128]{2,1,0:T(4,128)S(1)}) custom-call(s32[8192]{0:T(1024)S(1)} %bitcast.73, bf16[16,3,224,384]{3,2,1,0:T(8,128)(2,1)} %all-to-all-done.fields_ref, f32[16,128]{1,0:T(8,128)S(1)} %get-tuple-element.134.coef_ref, f32[4,4,128]{2,1,0:T(4,128)S(1)} %get-tuple-element.65.before_ref, ...), custom_call_target="tpu_custom_call" | custom-call | flops 16777216 | bytes 31981568 | tf_op jit(solution)/shard_map/cond/branch_0_fun/sens_block/pallas_call | solution.py:323
  233.7 12.1 %sens_block.14 = (f32[8192,128]{1,0:T(8,128)}, f32[4,4,128]{2,1,0:T(4,128)S(1)}) custom-call(s32[8192]{0:T(1024)S(1)} %bitcast.74, bf16[16,3,224,384]{3,2,1,0:T(8,128)(2,1)} %all-to-all-done.fields_ref, f32[16,128]{1,0:T(8,128)S(1)} %get-tuple-element.135.coef_ref, f32[4,4,128]{2,1,0:T(4,128)S(1)} %get-tuple-element.66.before_ref, ...), custom_call_target="tpu_custom_call" | custom-call | flops 16777216 | bytes 31981568 | tf_op jit(solution)/shard_map/cond/branch_0_fun/sens_block/pallas_call | solution.py:323
  245.8 16.1 %all-to-all-done.1.fields_ref = bf16[16,3,224,128]{3,2,1,0:T(8,128)(2,1)S(1)} async-done(((bf16[16,3,224,128]{3,2,1,0:T(8,128)(2,1)}), bf16[16,3,224,128]{3,2,1,0:T(8,128)(2,1)S(1)}, u32[]{:S(2)}, u32[]{:S(2)}) %all-to-all-start.1) | async-done | bytes 2752544 | tf_op jit(solution)/shard_map/cond/branch_0_fun/all_to_all | solution.py:520
  261.9 8.9 %sens_block.15 = (f32[8192,128]{1,0:T(8,128)S(1)}, f32[1,16,128]{2,1,0:T(8,128)S(1)}) custom-call(s32[8192]{0:T(1024)S(1)} %bitcast.75, bf16[16,3,224,128]{3,2,1,0:T(8,128)(2,1)S(1)} %all-to-all-done.1.fields_ref, f32[16,128]{1,0:T(8,128)S(1)} %get-tuple-element.136.coef_ref, f32[1,16,128]{2,1,0:T(8,128)S(1)} %bitcast.87, ...), custom_call_target="tpu_custom_call" | custom-call | flops 16777216 | bytes 31981568 | tf_op jit(solution)/shard_map/cond/branch_0_fun/sens_block/pallas_call | solution.py:323
  270.8 0.8 collective-permute-start.4
  271.7 0.8 collective-permute-done.4
  272.5 4.2 %collective-permute-start.5 = (f32[1,16,128]{2,1,0:T(8,128)S(1)}, f32[1,16,128]{2,1,0:T(8,128)S(1)}, u32[]{:S(2)}, u32[]{:S(2)}) collective-permute-start(f32[1,16,128]{2,1,0:T(8,128)S(1)} %add.85), channel_id=1, source_target_pairs={{0,2},{1,3},{2,0},{3,1},{4,6},{5,7},{6,4},{7,5},{8,10},{9,11},{10,... | collective-permute-start | bytes 24584 | tf_op jit(solution)/shard_map/cond/branch_0_fun/ppermute | solution.py:440
  276.7 1.6 collective-permute-done.5
  278.4 8.3 %collective-permute-start.8 = (f32[1,16,128]{2,1,0:T(8,128)S(1)}, f32[1,16,128]{2,1,0:T(8,128)S(1)}, u32[]{:S(2)}, u32[]{:S(2)}) collective-permute-start(f32[1,16,128]{2,1,0:T(8,128)S(1)} %add.86), channel_id=1, source_target_pairs={{0,12},{1,13},{2,14},{3,15},{4,8},{5,9},{6,10},{7,11},{8,4},{9,5},... | collective-permute-start | bytes 24584 | tf_op jit(solution)/shard_map/cond/branch_0_fun/ppermute | solution.py:440
  286.7 1.0 collective-permute-start.7
  287.7 0.6 collective-permute-start.6
  288.3 0.1 collective-permute-done.8
  288.3 2.9 collective-permute-done.7
  291.3 0.1 collective-permute-done.6
  291.4 8.5 %scaled.3 = (bf16[2048,4,512]{2,1,0:T(4,128)(2,1)}, f32[4,128]{1,0:T(4,128)}) custom-call(f32[16,128]{1,0:T(8,128)S(1)} %bitcast.84, f32[16,128]{1,0:T(8,128)S(1)} %add_bitcast_fusion.1.theirs_ref, f32[8192,128]{1,0:T(8,128)} %get-tuple-element.69.refs_0_, f32[8192,128]{1,0:T(8,128)} %get-tuple-element.70.refs_1_, f32[8192,128]{1,0:T(8,128)} %get-tuple-element.71.refs_2_, ...), custom_call_target="tpu_custom_call" | custom-call | tf_op jit(solution)/shard_map/cond/branch_0_fun/scaled/pallas_call | solution.py:411
  (14 shorter events, 0.2 us)
Async XLA Ops:
  0.6 10.2 %copy-start = (s32[2048,4]{0,1:T(4,128)S(1)}, s32[2048,4]{0,1:T(4,128)}, u32[]{:S(2)}) copy-start(s32[2048,4]{0,1:T(4,128)} %param.14) | copy-start | bytes 98308
  0.6 10.2 %copy-start.1 = (f32[512]{0:T(512)S(1)}, f32[512]{0:T(512)}, u32[]{:S(2)}) copy-start(f32[512]{0:T(512)} %param.13) | copy-start | bytes 6148
  0.7 10.2 %copy-start.2 = (f32[512]{0:T(512)S(1)}, f32[512]{0:T(512)}, u32[]{:S(2)}) copy-start(f32[512]{0:T(512)} %param.12) | copy-start | bytes 6148
  0.7 10.2 %copy-start.3 = (f32[512]{0:T(512)S(1)}, f32[512]{0:T(512)}, u32[]{:S(2)}) copy-start(f32[512]{0:T(512)} %param.10) | copy-start | bytes 6148
  0.7 10.2 %copy-start.4 = (f32[512]{0:T(512)S(1)}, f32[512]{0:T(512)}, u32[]{:S(2)}) copy-start(f32[512]{0:T(512)} %param.11) | copy-start | bytes 6148
  10.8 194.9 %all-to-all-start = ((bf16[16,3,224,384]{3,2,1,0:T(8,128)(2,1)}), bf16[16,3,224,384]{3,2,1,0:T(8,128)(2,1)}, u32[]{:S(2)}, u32[]{:S(2)}) async-start(bf16[16,3,224,384]{3,2,1,0:T(8,128)(2,1)} %get-tuple-element.52), calls=%async_computation | async-start | bytes 16515072 | tf_op jit(solution)/shard_map/cond/branch_0_fun/all_to_all | solution.py:520
  26.2 2.9 collective-permute-start
  30.5 60.7 %collective-permute-start.1 = (bf16[4,3,48,512]{3,2,1,0:T(8,128)(2,1)S(1)}, bf16[4,3,48,512]{3,2,1,0:T(8,128)(2,1)S(1)}, u32[]{:S(2)}, u32[]{:S(2)}) collective-permute-start(bf16[4,3,48,512]{3,2,1,0:T(8,128)(2,1)S(1)} %dynamic-slice_bitcast_fusion.1), channel_id=1, source_target_pairs={{0,2},{1,3},{2,0},{3,1},{4,6},{5,7},{6,4},{7,5},{8,10},{9,11},{10,... | collective-permute-start | bytes 1769480 | tf_op jit(solution)/shard_map/cond/branch_0_fun/ppermute | solution.py:475
  91.4 67.2 %collective-permute-start.2 = (bf16[2,3,48,512]{3,2,1,0:T(8,128)(2,1)S(1)}, bf16[2,3,48,512]{3,2,1,0:T(8,128)(2,1)S(1)}, u32[]{:S(2)}, u32[]{:S(2)}) collective-permute-start(bf16[2,3,48,512]{3,2,1,0:T(8,128)(2,1)S(1)} %dynamic-slice_bitcast_fusion.2), channel_id=1, source_target_pairs={{0,4},{1,5},{2,6},{3,7},{4,0},{5,1},{6,2},{7,3},{8,12},{9,13},{10,... | collective-permute-start | bytes 884744 | tf_op jit(solution)/shard_map/cond/branch_0_fun/ppermute | solution.py:475
  158.6 47.1 %collective-permute-start.3 = (bf16[1,3,48,512]{3,2,1,0:T(8,128)(2,1)S(1)}, bf16[1,3,48,512]{3,2,1,0:T(8,128)(2,1)S(1)}, u32[]{:S(2)}, u32[]{:S(2)}) collective-permute-start(bf16[1,3,48,512]{3,2,1,0:T(8,128)(2,1)S(1)} %constant_dynamic-slice_fusion), channel_id=1, source_target_pairs={{0,8},{1,9},{2,10},{3,11},{4,12},{5,13},{6,14},{7,15},{8,0},{9,1},... | collective-permute-start | bytes 442376 | tf_op jit(solution)/shard_map/cond/branch_0_fun/ppermute | solution.py:475
  205.7 56.2 %all-to-all-start.1 = ((bf16[16,3,224,128]{3,2,1,0:T(8,128)(2,1)}), bf16[16,3,224,128]{3,2,1,0:T(8,128)(2,1)S(1)}, u32[]{:S(2)}, u32[]{:S(2)}) async-start(bf16[16,3,224,128]{3,2,1,0:T(8,128)(2,1)} %send_order.5), calls=%async_computation.1 | async-start | bytes 5505024 | tf_op jit(solution)/shard_map/cond/branch_0_fun/all_to_all | solution.py:520
  270.8 1.7 collective-permute-start.4
  272.5 5.9 %collective-permute-start.5 = (f32[1,16,128]{2,1,0:T(8,128)S(1)}, f32[1,16,128]{2,1,0:T(8,128)S(1)}, u32[]{:S(2)}, u32[]{:S(2)}) collective-permute-start(f32[1,16,128]{2,1,0:T(8,128)S(1)} %add.85), channel_id=1, source_target_pairs={{0,2},{1,3},{2,0},{3,1},{4,6},{5,7},{6,4},{7,5},{8,10},{9,11},{10,... | collective-permute-start | bytes 24584 | tf_op jit(solution)/shard_map/cond/branch_0_fun/ppermute | solution.py:440
  278.4 10.0 %collective-permute-start.8 = (f32[1,16,128]{2,1,0:T(8,128)S(1)}, f32[1,16,128]{2,1,0:T(8,128)S(1)}, u32[]{:S(2)}, u32[]{:S(2)}) collective-permute-start(f32[1,16,128]{2,1,0:T(8,128)S(1)} %add.86), channel_id=1, source_target_pairs={{0,12},{1,13},{2,14},{3,15},{4,8},{5,9},{6,10},{7,11},{8,4},{9,5},... | collective-permute-start | bytes 24584 | tf_op jit(solution)/shard_map/cond/branch_0_fun/ppermute | solution.py:440
  286.7 4.5 %collective-permute-start.7 = (f32[1,16,128]{2,1,0:T(8,128)S(1)}, f32[1,16,128]{2,1,0:T(8,128)S(1)}, u32[]{:S(2)}, u32[]{:S(2)}) collective-permute-start(f32[1,16,128]{2,1,0:T(8,128)S(1)} %add.86), channel_id=1, source_target_pairs={{0,8},{1,9},{2,10},{3,11},{4,12},{5,13},{6,14},{7,15},{8,0},{9,1},... | collective-permute-start | bytes 24584 | tf_op jit(solution)/shard_map/cond/branch_0_fun/ppermute | solution.py:440
  287.7 3.7 %collective-permute-start.6 = (f32[1,16,128]{2,1,0:T(8,128)S(1)}, f32[1,16,128]{2,1,0:T(8,128)S(1)}, u32[]{:S(2)}, u32[]{:S(2)}) collective-permute-start(f32[1,16,128]{2,1,0:T(8,128)S(1)} %add.86), channel_id=1, source_target_pairs={{0,4},{1,5},{2,6},{3,7},{4,0},{5,1},{6,2},{7,3},{8,12},{9,13},{10,... | collective-permute-start | bytes 24584 | tf_op jit(solution)/shard_map/cond/branch_0_fun/ppermute | solution.py:440
